TPU v7x, 32 devices: a whole 2x2x4 slice. The times are simulated.
32 devices in a mesh: groups: 2 (over x), ctx: 16 (over z, y, core).
Axes of the slice: x: 2, y: 2, z: 4, core: 2. Of those that a mesh axis runs over, the one named last changes fastest.
Arguments:
- queries: bfloat16 [96, 4096], P(('groups', 'ctx')), parts along dimension 0, may hold values from -200 to 200
- cache_keys: bfloat16 [4096, 512], P(('groups', 'ctx')), parts along dimension 0, may hold values from -6 to 6
- cache_values: bfloat16 [4096, 512], P(('groups', 'ctx')), parts along dimension 0, may hold values from -6 to 6
- new_keys: bfloat16 [96, 512], P(('groups', 'ctx')), parts along dimension 0, may hold values from -6 to 6
- new_values: bfloat16 [96, 512], P(('groups', 'ctx')), parts along dimension 0, may hold values from -6 to 6
- cache_lengths: int32 [32], P(('groups', 'ctx')), parts along dimension 0, may hold values from 0 to 128, as said below
- residual_in: bfloat16 [96, 2048], P(('groups', 'ctx')), parts along dimension 0, may hold values from -6 to 6
- out_weight: bfloat16 [4096, 2048], P('ctx'), may hold values from -3 to 3
- norm_gain: bfloat16 [2048], replicated, may hold values from 0.25 to 1.75
- expert_gate: bfloat16 [16, 2048, 768], P('ctx'), may hold values from -0.125 to 0.125
- expert_up: bfloat16 [16, 2048, 768], P('ctx'), may hold values from -0.125 to 0.125
- expert_down: bfloat16 [16, 768, 2048], P('ctx'), may hold values from -0.21875 to 0.21875
- expert_ids: int32 [96, 8], P(('groups', 'ctx')), parts along dimension 0, may hold values from 0 to 15, all different within a row; in each aligned block of 3 rows (0 to 2, 3 to 5, ...) at most 3 rows name the same one
- expert_weights: float32 [96, 8], P(('groups', 'ctx')), parts along dimension 0, may hold values from 0.03 to 0.4
Outputs:
- layer_out: bfloat16 [96, 2048], P(('groups', 'ctx')), parts along dimension 0
There are 2 independent parts, one for each index of `groups`. A program takes and returns all parts, laid end to end along the dimension named above; an argument that names none is the same for every part. Nothing has to cross between parts.
Inputs may be any that keep to these rules, and one draw needn't show every extreme that they name: `cache_lengths`: some shard in every draw is full, with 128 live positions. `expert_ids`: within one block of 3 rows no expert is named more than 3 times, a bound that some block reaches.
All inputs are finite; a program needn't handle non-finite values.
Results may differ from a plain program's by a relative error of at most 0.01.
Values may be sent and summed in bfloat16 or wider, within the bound.
A program may use at most 64 MiB of HBM per device.

v0:
```python
import jax
import jax.numpy as jnp
from jax import lax
from jax.sharding import PartitionSpec as P

HEADS = 32
KV_HEADS = 4
HEAD_DIM = 128
TOP = 8


MASKED = -1e30
epsilon = 1e-06


def local(
    queries,
    cache_keys,
    cache_values,
    new_keys,
    new_values,
    cache_lengths,
    residual_in,
    out_weight,
    norm_gain,
    expert_gate,
    expert_up,
    expert_down,
    expert_ids,
    expert_weights,
):
    shards = lax.axis_size("ctx")
    device = lax.axis_index("ctx")
    rows_dev = residual_in.shape[0]
    capacity = max(2, 2 * rows_dev * TOP // shards)
    group_size = HEADS // KV_HEADS
    whole_queries = lax.all_gather(queries, "ctx", axis=0, tiled=True)
    all_rows = whole_queries.shape[0]
    query_heads = whole_queries.reshape(all_rows, KV_HEADS, group_size, HEAD_DIM)
    local_cache = cache_keys.shape[0]
    key_rows = jnp.concatenate([cache_keys, new_keys], 0).reshape(
        local_cache + rows_dev, KV_HEADS, HEAD_DIM
    )
    value_rows = jnp.concatenate([cache_values, new_values], 0).reshape(
        local_cache + rows_dev, KV_HEADS, HEAD_DIM
    )
    slot_ids = jnp.arange(local_cache + rows_dev, dtype=jnp.int32)
    span_pos = device * rows_dev + slot_ids - local_cache
    row_ids = jnp.arange(all_rows, dtype=jnp.int32)
    usable = jnp.where(
        slot_ids[None, :] < local_cache,
        (slot_ids < cache_lengths[0])[None, :],
        span_pos[None, :] <= row_ids[:, None],
    )
    scores = jnp.einsum(
        "rkgd,nkd->kgrn", query_heads, key_rows, preferred_element_type=jnp.float32
    ) * HEAD_DIM ** (-0.5)
    scores = jnp.where(usable, scores, MASKED)
    maxima = jnp.max(scores, axis=-1)
    exp_weights = jnp.where(usable, jnp.exp(scores - maxima[..., None]), 0.0)
    totals = jnp.sum(exp_weights, axis=-1)
    numerators = jnp.einsum(
        "kgrn,nkd->rkgd",
        exp_weights.astype(jnp.bfloat16),
        value_rows,
        preferred_element_type=jnp.float32,
    ).reshape(all_rows, HEADS, HEAD_DIM)
    maxima = maxima.transpose(2, 0, 1).reshape(all_rows, HEADS)
    totals = totals.transpose(2, 0, 1).reshape(all_rows, HEADS)
    largest = lax.pmax(maxima, "ctx")
    rescale = jnp.exp(maxima - largest)
    denoms = lax.psum(totals * rescale, "ctx")
    weighted = (numerators * (rescale / denoms)[..., None]).reshape(all_rows, HEADS * HEAD_DIM)
    columns = lax.psum_scatter(weighted, "ctx", scatter_dimension=1, tiled=True).astype(
        jnp.bfloat16
    )
    projected = lax.psum_scatter(
        jnp.dot(columns, out_weight, preferred_element_type=jnp.float32),
        "ctx",
        scatter_dimension=0,
        tiled=True,
    )
    state = residual_in.astype(jnp.float32) + projected
    normed = (
        state
        * lax.rsqrt(jnp.mean(state * state, axis=1, keepdims=True) + epsilon)
        * norm_gain.astype(jnp.float32)
    ).astype(jnp.bfloat16)
    n_slots = shards * capacity
    flat_ids = expert_ids.reshape(-1)
    places = jnp.arange(flat_ids.shape[0], dtype=jnp.int32)
    earlier = (flat_ids[:, None] == flat_ids[None, :]) & (places[None, :] < places[:, None])
    slot_of = flat_ids * capacity + jnp.sum(earlier.astype(jnp.int32), axis=1)
    one_hot = (slot_of[:, None] == jnp.arange(n_slots, dtype=jnp.int32)[None, :]).astype(
        jnp.float32
    )
    dispatch_map = one_hot.reshape(rows_dev, TOP, n_slots).sum(1)
    outgoing = (
        jnp.dot(dispatch_map.T.astype(jnp.bfloat16), normed, preferred_element_type=jnp.float32)
        .astype(jnp.bfloat16)
        .reshape(shards, capacity, normed.shape[1])
    )
    received = lax.all_to_all(outgoing, "ctx", split_axis=0, concat_axis=0, tiled=True)
    gate_out = jnp.einsum(
        "scd,df->scf", received, expert_gate[0], preferred_element_type=jnp.float32
    )
    up_out = jnp.einsum("scd,df->scf", received, expert_up[0], preferred_element_type=jnp.float32)
    activated = (jax.nn.silu(gate_out) * up_out).astype(jnp.bfloat16)
    expert_out = jnp.einsum(
        "scf,fd->scd", activated, expert_down[0], preferred_element_type=jnp.float32
    ).astype(jnp.bfloat16)
    back = lax.all_to_all(expert_out, "ctx", split_axis=0, concat_axis=0, tiled=True)
    combine_map = (
        (one_hot * expert_weights.reshape(-1)[:, None]).reshape(rows_dev, TOP, n_slots).sum(1)
    )
    expert_sum = jnp.dot(
        combine_map,
        back.reshape(n_slots, normed.shape[1]).astype(jnp.float32),
        precision=lax.Precision.HIGHEST,
    )
    return (state + expert_sum).astype(jnp.bfloat16)


def solution(mesh):
    placed = (
        P(("groups", "ctx"), None),
        P(("groups", "ctx"), None),
        P(("groups", "ctx"), None),
        P(("groups", "ctx"), None),
        P(("groups", "ctx"), None),
        P(("groups", "ctx")),
        P(("groups", "ctx"), None),
        P("ctx", None),
        P(),
        P("ctx", None, None),
        P("ctx", None, None),
        P("ctx", None, None),
        P(("groups", "ctx"), None),
        P(("groups", "ctx"), None),
    )
    return jax.shard_map(
        local, mesh=mesh, in_specs=placed, out_specs=P(("groups", "ctx"), None), check_vma=False
    )
```

profile of v0, /device:TPU:0, one launch (start us, length us, event | category | flops | bytes accessed | tf_op | source)
XLA Modules:
  0.0 358.9 jit_solution(11415697979822261193)
XLA Ops:
  7.3 0.6 add_add_fusion
  7.9 0.6 iota_compare_fusion.3
  8.5 0.9 pad_maximum_fusion.1
  9.5 0.9 pad_maximum_fusion
  10.5 0.1 reshape.87
  10.6 26.4 %all-gather = bf16[16,3,4096]{2,1,0:T(4,128)(2,1)} all-gather(bf16[1,3,4096]{2,1,0:T(4,128)(2,1)} %bitcast.55), channel_id=1, replica_groups=mesh['groups'=2,'ctx'=16] {'ctx'}, dimensions={0}, use_global_device_ids=true | all-gather | bytes 417792 | tf_op jit(solution)/shard_map/all_gather | solution.py:37
  37.0 2.2 reshape.89
  39.2 0.7 fusion.36
  39.9 2.6 fusion.46
  42.4 57.8 %pmax.7 = f32[48,32]{0,1:T(8,128)S(1)} all-reduce(f32[48,32]{0,1:T(8,128)S(1)} %bitcast.53), channel_id=1, replica_groups=mesh['groups'=2,'ctx'=16] {'ctx'}, use_global_device_ids=true, to_apply=%region_1.2 | all-reduce | flops 1536 | bytes 12288 | tf_op jit(solution)/shard_map/pmax | solution.py:70
  100.3 2.1 fusion.10
  102.3 0.4 convolution_bitcast_fusion
  102.8 1.1 copy.35
  103.9 57.6 %psum.7 = f32[48,32]{0,1:T(8,128)S(1)} all-reduce(f32[48,32]{0,1:T(8,128)S(1)} %bitcast_multiply_fusion.1), channel_id=1, replica_groups=mesh['groups'=2,'ctx'=16] {'ctx'}, use_global_device_ids=true, to_apply=%region_3.4 | all-reduce | flops 1536 | bytes 12288 | tf_op jit(solution)/shard_map/psum | solution.py:72
  161.6 0.3 mul.72
  161.9 3.1 bitcast_multiply_fusion
  165.2 0.2 convert_reduce_fusion.1
  165.5 53.5 %reduce-scatter.2.cloned.1.call-done = f32[48,256]{1,0:T(8,128)} async-done(((f32[48,4096]{1,0:T(8,128)}), f32[48,256]{1,0:T(8,128)}) %reduce-scatter.2.cloned.1.call-update) | async-done | bytes 49168 | tf_op jit(solution)/shard_map/reduce_scatter | solution.py:74
  218.9 2.3 fusion.37
  221.3 0.6 dynamic-slice
  222.5 0.7 convert_reduce_fusion
  223.2 88.9 %all-reduce.3.cloned.1.call-done = f32[48,2048]{1,0:T(8,128)} async-done(((f32[48,2048]{1,0:T(8,128)}), f32[48,2048]{1,0:T(8,128)}) %all-reduce.3.cloned.1.call-update) | async-done | bytes 393232
  312.2 1.0 multiply_reduce_fusion
  313.2 1.2 convolution_convert_fusion
  314.4 0.8 reshape.93
  315.2 13.8 %all_to_all.10 = bf16[16,3,2048]{2,1,0:T(4,128)(2,1)S(1)} all-to-all(bf16[16,3,2048]{2,1,0:T(4,128)(2,1)} %reshape.93), channel_id=1, replica_groups=mesh['groups'=2,'ctx'=16] {'ctx'}, dimensions={0} | all-to-all | bytes 393216 | tf_op jit(solution)/shard_map/all_to_all | solution.py:103
  329.0 2.6 fusion.4
  331.6 3.9 %fusion.6 = bf16[16,3,2048]{2,0,1:T(8,128)(2,1)} fusion(bf16[1,768,2048]{2,1,0:T(8,128)(2,1)S(1)} %copy-done, bf16[1,2048,768]{2,1,0:T(8,128)(2,1)} %param.24, f32[16,3,768]{2,0,1:T(8,128)S(1)} %fusion.4, bf16[16,3,2048]{2,1,0:T(4,128)(2,1)S(1)} %all_to_all.10), kind=kOutput, calls=%fused_computation.6 | convolution fusion | flops 302309376 | bytes 6832128 | tf_op jit(solution)/shard_map/scf,fd->scd/dot_general | solution.py:109
  335.5 1.1 copy.39
  336.6 12.8 %all_to_all.11 = bf16[16,3,2048]{2,1,0:T(4,128)(2,1)S(1)} all-to-all(bf16[16,3,2048]{2,1,0:T(4,128)(2,1)S(1)} %copy.39), channel_id=1, replica_groups=mesh['groups'=2,'ctx'=16] {'ctx'}, dimensions={0} | all-to-all | bytes 393216 | tf_op jit(solution)/shard_map/all_to_all | solution.py:112
  349.4 0.8 reshape.94
  350.3 1.8 fusion.9
  (27 shorter events, 0.5 us)
Async XLA Ops:
  6.5 325.0 %copy-start = (bf16[1,768,2048]{2,1,0:T(8,128)(2,1)S(1)}, bf16[1,768,2048]{2,1,0:T(8,128)(2,1)}, u32[]{:S(2)}) copy-start(bf16[1,768,2048]{2,1,0:T(8,128)(2,1)} %param.25) | copy-start | bytes 9437188
  6.5 212.4 %reduce-scatter.2.cloned.1.call-start = ((), (), s32[]{:S(2)}) async-start(), calls=%async_computation.3 | async-start | bytes 835584 | tf_op jit(solution)/shard_map/reduce_scatter | solution.py:74
  100.3 2.1 copy-start.1
  161.9 3.2 copy-start.3
  165.0 56.2 %copy-start.4 = (bf16[2048]{0:T(1024)(128)(2,1)S(1)}, bf16[2048]{0:T(1024)(128)(2,1)}, u32[]{:S(2)}) copy-start(bf16[2048]{0:T(1024)(128)(2,1)} %param.22) | copy-start | bytes 12292
  165.0 56.3 %copy-start.6 = (u32[32]{0:T(128)S(1)}, u32[32]{0:T(128)}, u32[]{:S(2)}) copy-start(u32[32]{0:T(128)} %constant.43) | copy-start | bytes 388
  165.0 57.5 %copy-start.5 = (f32[3,8]{1,0:T(4,128)S(1)}, f32[3,8]{1,0:T(4,128)}, u32[]{:S(2)}) copy-start(f32[3,8]{1,0:T(4,128)} %param.27) | copy-start | bytes 292
  165.0 147.1 %copy-start.2 = (bf16[3,2048]{1,0:T(4,128)(2,1)S(1)}, bf16[3,2048]{1,0:T(4,128)(2,1)}, u32[]{:S(2)}) copy-start(bf16[3,2048]{1,0:T(4,128)(2,1)} %param.20) | copy-start | bytes 36868
  165.1 147.1 %all-reduce.3.cloned.1.call-start = ((), (), s32[]{:S(2)}) async-start(), calls=%async_computation.4 | async-start | bytes 786432
Sparse Core Ops, SparseCore 0:
  165.2 53.7 reduce-scatter.1
  222.6 89.4 all-reduce.2
where the time goes:
time: 360 us; the launch traced here: 359 us
  blocking collectives  168 us (47%)
  waiting for transfers between devices  142 us (39%)
  between operations  15 us (4%)
  matrix products  14.8 us (4%)
  other arithmetic  10.8 us (3%)
  local copies, waits for them, and re-layouts  7.41 us (2%)
    unnamed x3, waiting for transfers between devices  89 us
    pmax x1, blocking collectives, local(): largest = lax.pmax(maxima, 'ctx')  57.8 us
    psum x1, blocking collectives, local(): denoms = lax.psum(totals * rescale, 'ctx')  57.6 us
    reduce_scatter x1, waiting for transfers between devices, local(): lax.psum_scatter(weighted, 'ctx', scatter_dimension=1, tiled=True)  53.5 us
    all_gather x1, blocking collectives, local(): whole_queries = lax.all_gather(queries, 'ctx', axis=0, tiled=True)  26.4 us
    all_to_all x1, blocking collectives, local(): lax.all_to_all(outgoing, 'ctx', split_axis=0, concat_axis=0, tiled=True)  13.8 us
    all_to_all x1, blocking collectives, local(): lax.all_to_all(expert_out, 'ctx', split_axis=0, concat_axis=0, tiled=True)  12.8 us
  transfers between devices with their start and end apart: 2, of which 2 were waited for; matrix products, arithmetic and copies ran while one was open for 0% of the time, Pallas kernels for 0%

commit v1 on v0

--- a/solution.py
+++ b/solution.py
@@ -1,6 +1,10 @@
+import functools
+
 import jax
 import jax.numpy as jnp
 from jax import lax
+from jax.experimental import pallas as pl
+from jax.experimental.pallas import tpu as pltpu
 from jax.sharding import PartitionSpec as P
 
 HEADS = 32
@@ -13,7 +17,7 @@
 epsilon = 1e-06
 
 
-def local(
+def plain(
     queries,
     cache_keys,
     cache_values,
@@ -121,6 +125,448 @@
     return (state + expert_sum).astype(jnp.bfloat16)
 
 
+LANES = 128
+SUB = 8
+HALF = SUB // 2
+MESH = pl.DeviceIdType.MESH
+F32 = jnp.float32
+BF16 = jnp.bfloat16
+Q, K, V, NEW, NUM, STAT, PROJ, ROWS, BACK = range(9)
+
+
+def fits(shards, rows_dev, width, capacity, experts_dev):
+    team = shards // KV_HEADS
+    if shards % KV_HEADS or team == 0 or (HEADS // KV_HEADS) % team:
+        return False
+    pair = HEADS // KV_HEADS // team
+    return (
+        experts_dev == 1
+        and HEAD_DIM == LANES
+        and shards * SUB == LANES
+        and rows_dev < HALF
+        and pair * rows_dev <= SUB
+        and capacity >= rows_dev
+        and width % (4 * LANES) == 0
+    )
+
+
+def layer_kernel(
+    shards,
+    q_ref,
+    ck_ref,
+    cv_ref,
+    nk_ref,
+    nv_ref,
+    len_ref,
+    res_ref,
+    wo_ref,
+    gain_ref,
+    wg_ref,
+    wu_ref,
+    wd_ref,
+    ids_ref,
+    ew_ref,
+    out_ref,
+    wo,
+    wg,
+    wu,
+    wd,
+    q_wide,
+    q_send,
+    q_recv,
+    q_heads,
+    k_all,
+    v_all,
+    new_wide,
+    new_send,
+    new_recv,
+    num_send,
+    num_recv,
+    stat_send,
+    stat_recv,
+    proj_send,
+    proj_recv,
+    res_wide,
+    gain_wide,
+    ids_wide,
+    ew_wide,
+    mix,
+    row_send,
+    row_recv,
+    x_all,
+    act,
+    back_send,
+    back_recv,
+    load_sem,
+    send_sem,
+    recv_sem,
+):
+    me = lax.axis_index("ctx")
+    team = shards // KV_HEADS
+    pair = HEADS // KV_HEADS // team
+    rows_dev, width = res_ref.shape
+    chunks = width // LANES
+    cache = ck_ref.shape[0]
+    head, mate = me // team, me % team
+
+    barrier = pltpu.get_barrier_semaphore()
+
+    def greet(step, carry):
+        pl.semaphore_signal(
+            barrier, inc=1, device_id={"ctx": lax.rem(me + step, shards)}, device_id_type=MESH
+        )
+        return carry
+
+    lax.fori_loop(1, shards, greet, 0)
+
+    own_lanes = pl.ds(pl.multiple_of(head * LANES, LANES), LANES)
+    loads = [
+        pltpu.make_async_copy(ck_ref.at[:, own_lanes], k_all.at[head], load_sem.at[0]),
+        pltpu.make_async_copy(cv_ref.at[:, own_lanes], v_all.at[head], load_sem.at[1]),
+        pltpu.make_async_copy(wo_ref, wo, load_sem.at[2]),
+        pltpu.make_async_copy(wg_ref.at[0], wg, load_sem.at[3]),
+        pltpu.make_async_copy(wu_ref.at[0], wu, load_sem.at[4]),
+        pltpu.make_async_copy(wd_ref.at[0], wd, load_sem.at[5]),
+    ]
+    for load in loads:
+        load.start()
+
+    q_wide[...] = jnp.zeros_like(q_wide)
+    for one in range(HEADS):
+        kv, rest = divmod(one, HEADS // KV_HEADS)
+        who, which = divmod(rest, pair)
+        q_wide[kv, pl.ds(who * SUB + which * rows_dev, rows_dev), :] = q_ref[
+            :, one * LANES : (one + 1) * LANES
+        ].astype(F32)
+    q_send[...] = q_wide[...].astype(BF16)
+    new_wide[...] = jnp.zeros_like(new_wide)
+    live = jnp.full((1, LANES), len_ref[0], jnp.int32).astype(F32)
+    for kv in range(KV_HEADS):
+        lanes = slice(kv * LANES, (kv + 1) * LANES)
+        new_wide[kv, 0:rows_dev, :] = nk_ref[:, lanes].astype(F32)
+        new_wide[kv, rows_dev : rows_dev + 1, :] = live
+        new_wide[kv, SUB : SUB + rows_dev, :] = nv_ref[:, lanes].astype(F32)
+    new_send[...] = new_wide[...].astype(BF16)
+
+    def remote(kind, src, dst, target, source):
+        return pltpu.make_async_remote_copy(
+            src_ref=src,
+            dst_ref=dst,
+            send_sem=send_sem.at[kind, target],
+            recv_sem=recv_sem.at[kind, source],
+            device_id={"ctx": target},
+            device_id_type=MESH,
+        )
+
+    def column(step):
+        other = lax.rem(head + step, KV_HEADS)
+        return other, other * team + mate
+
+    def key_copies(other, target, source_head):
+        lanes = pl.ds(pl.multiple_of(other * LANES, LANES), LANES)
+        source = source_head * team + mate
+        return (
+            remote(K, ck_ref.at[:, lanes], k_all.at[source_head], target, source),
+            remote(V, cv_ref.at[:, lanes], v_all.at[source_head], target, source),
+            remote(NEW, new_send.at[other], new_recv.at[source_head], target, source),
+        )
+
+    pl.semaphore_wait(barrier, shards - 1)
+
+    def peers(body):
+        def step_body(step, carry):
+            body(lax.rem(me + step, shards))
+            return carry
+
+        lax.fori_loop(1, shards, step_body, 0)
+
+    def q_copy(target, source):
+        return remote(Q, q_send.at[target // team], q_recv.at[source], target, source)
+
+    for step in range(1, KV_HEADS):
+        for copy in key_copies(*column(step), head):
+            copy.start()
+    peers(lambda other: q_copy(other, me).start())
+
+    q_recv[me] = q_send[head]
+    new_recv[head] = new_send[head]
+
+    res_wide[...] = jnp.zeros_like(res_wide)
+    for c in range(chunks):
+        lanes = slice(c * LANES, (c + 1) * LANES)
+        res_wide[c * HALF : c * HALF + rows_dev, :] = res_ref[:, lanes].astype(F32)
+        gain_wide[c * HALF : (c + 1) * HALF, :] = jnp.broadcast_to(
+            gain_ref[:, lanes].astype(F32), (HALF, LANES)
+        )
+    ids_wide[...] = jnp.full_like(ids_wide, -1)
+    ew_wide[...] = jnp.zeros_like(ew_wide)
+    for half in range(2):
+        at = slice(half * HALF, half * HALF + rows_dev)
+        ids_wide[at, :] = ids_ref[...]
+        ew_wide[at, :] = ew_ref[...]
+    for e in range(shards):
+        share = jnp.where(ids_wide[...] == e, ew_wide[...], 0.0)
+        mix[e] = jnp.broadcast_to(jnp.sum(share, axis=1, keepdims=True), (SUB, LANES))
+
+    peers(lambda other: q_copy(me, other).wait_recv())
+    gathered = q_recv[...].astype(F32).reshape(shards, team, SUB, LANES)
+    for one in range(team):
+        q_heads[one] = gathered[:, one].reshape(shards * SUB, LANES).astype(BF16)
+    loads[0].wait()
+    loads[1].wait()
+    for step in range(1, KV_HEADS):
+        other, _ = column(step)
+        for copy in key_copies(head, me, other):
+            copy.wait_recv()
+
+    n_cache = KV_HEADS * cache
+    n_new = KV_HEADS * SUB
+    fresh = new_recv[...].astype(F32)
+    new_k = fresh[:, 0:SUB].reshape(n_new, LANES).astype(BF16)
+    new_v = fresh[:, SUB : 2 * SUB].reshape(n_new, LANES).astype(BF16)
+    lengths = fresh[:, rows_dev : rows_dev + 1, :]
+    spot = lax.broadcasted_iota(jnp.int32, (KV_HEADS, cache, LANES), 1).astype(F32)
+    cache_ok = (spot < lengths).reshape(n_cache, LANES)
+    lane = lax.broadcasted_iota(jnp.int32, (n_new, LANES), 1)
+    place = lax.broadcasted_iota(jnp.int32, (n_new, LANES), 0)
+    row_of = (lane // SUB) * rows_dev + (lane % SUB) % rows_dev
+    key_at = place % SUB
+    span = ((place // SUB) * team + mate) * rows_dev + key_at
+    new_ok = (key_at < rows_dev) & (span <= row_of)
+    across = (((1,), (1,)), ((), ()))
+    down = (((0,), (0,)), ((), ()))
+    scale = HEAD_DIM ** (-0.5)
+    stat_row = lax.broadcasted_iota(jnp.int32, (SUB, LANES), 0)
+
+    def team_copies(target_mate, source_mate):
+        target, source = head * team + target_mate, head * team + source_mate
+        return (
+            remote(NUM, num_send.at[target_mate], num_recv.at[source_mate], target, source),
+            remote(STAT, stat_send.at[target_mate], stat_recv.at[source_mate], target, source),
+        )
+
+    def attend(step, carry):
+        to = lax.rem(mate + step, team)
+        queries = q_heads[to]
+        keys = k_all[...].reshape(n_cache, LANES)
+        old = lax.dot_general(keys, queries, across, preferred_element_type=F32) * scale
+        new = lax.dot_general(new_k, queries, across, preferred_element_type=F32) * scale
+        old = jnp.where(cache_ok, old, MASKED)
+        new = jnp.where(new_ok, new, MASKED)
+        top = jnp.maximum(
+            jnp.max(old, axis=0, keepdims=True), jnp.max(new, axis=0, keepdims=True)
+        )
+        old = jnp.where(cache_ok, jnp.exp(old - top), 0.0)
+        new = jnp.where(new_ok, jnp.exp(new - top), 0.0)
+        total = jnp.sum(old, axis=0, keepdims=True) + jnp.sum(new, axis=0, keepdims=True)
+        values = v_all[...].reshape(n_cache, LANES)
+        numer = lax.dot_general(values, old.astype(BF16), down, preferred_element_type=F32)
+        numer += lax.dot_general(new_v, new.astype(BF16), down, preferred_element_type=F32)
+        num_send[to] = numer.astype(BF16)
+        stat_send[to] = jnp.where(stat_row == 0, top, total)
+
+        @pl.when(step < team)
+        def _():
+            for copy in team_copies(to, mate):
+                copy.start()
+
+        return carry
+
+    lax.fori_loop(1, team + 1, attend, 0)
+    num_recv[mate] = num_send[mate]
+    stat_recv[mate] = stat_send[mate]
+    for step in range(1, team):
+        for copy in team_copies(mate, lax.rem(mate + step, team)):
+            copy.wait_recv()
+    tops = stat_recv[:, 0:1, :]
+    weight = jnp.exp(tops - jnp.max(tops, axis=0, keepdims=True))
+    weight = weight / jnp.sum(weight * stat_recv[:, 1:2, :], axis=0, keepdims=True)
+    attention = jnp.sum(num_recv[...].astype(F32) * weight, axis=0).astype(BF16)
+
+    n_tile = shards * SUB
+    tile_row = lax.broadcasted_iota(jnp.int32, (n_tile, LANES), 0)
+    tile_lane = lax.broadcasted_iota(jnp.int32, (n_tile, LANES), 1)
+    odd = (tile_row % SUB) >= HALF
+    own_row = tile_row % HALF
+    parts = []
+    for which in range(pair):
+        pick = (
+            (tile_row // SUB == tile_lane // SUB)
+            & (own_row < rows_dev)
+            & (tile_lane % SUB == which * rows_dev + own_row)
+        )
+        pick = jnp.where(pick, 1.0, 0.0).astype(BF16)
+        parts.append(
+            lax.dot_general(pick, attention, across, preferred_element_type=F32).astype(BF16)
+        )
+    columns = jnp.concatenate(parts, axis=1)
+
+    def to_blocks(ref, at, tile):
+        pieces = []
+        for j in range(2):
+            left = tile[:, 2 * j * LANES : (2 * j + 1) * LANES]
+            right = tile[:, (2 * j + 1) * LANES : (2 * j + 2) * LANES]
+            pieces.append(jnp.where(odd, right, left).reshape(shards, SUB, LANES))
+        ref[:, at * 2 * SUB : (at + 1) * 2 * SUB, :] = jnp.concatenate(pieces, axis=1).astype(BF16)
+
+    loads[2].wait()
+    wide = 4 * LANES
+    for at in range(width // wide):
+        tile = jnp.dot(columns, wo[:, at * wide : (at + 1) * wide], preferred_element_type=F32)
+        to_blocks(proj_send, at, tile)
+
+    def proj_copy(target, source):
+        return remote(PROJ, proj_send.at[target], proj_recv.at[source], target, source)
+
+    peers(lambda other: proj_copy(other, me).start())
+    proj_recv[me] = proj_send[me]
+    peers(lambda other: proj_copy(me, other).wait_recv())
+    state = res_wide[...] + jnp.sum(proj_recv[...].astype(F32), axis=0)
+    state = state.reshape(chunks // 2, SUB, LANES)
+    squares = jnp.sum(jnp.sum(state * state, axis=0), axis=1, keepdims=True)
+    squares = squares + jnp.concatenate([squares[HALF:], squares[:HALF]], axis=0)
+    normed = state * lax.rsqrt(squares / width + epsilon)[None]
+    normed = normed.reshape(chunks * HALF, LANES) * gain_wide[...]
+    row_send[...] = normed.astype(BF16)
+
+    def row_copy(target, source):
+        return remote(ROWS, row_send, row_recv.at[source], target, source)
+
+    peers(lambda other: row_copy(other, me).start())
+    row_recv[me] = row_send[...]
+    peers(lambda other: row_copy(me, other).wait_recv())
+
+    for at in range(chunks // 4):
+        both = row_recv[:, at * 2 * SUB : (at + 1) * 2 * SUB, :].astype(F32)
+        for j in range(2):
+            piece = both[:, j * SUB : (j + 1) * SUB].reshape(n_tile, LANES)
+            start = (4 * at + 2 * j) * LANES
+            x_all[:, start : start + LANES] = jnp.where(odd, 0.0, piece).astype(BF16)
+            x_all[:, start + LANES : start + 2 * LANES] = jnp.where(odd, piece, 0.0).astype(BF16)
+
+    def fold(part):
+        part = part.reshape(shards, SUB, part.shape[1])
+        turned = jnp.concatenate([part[:, HALF:], part[:, :HALF]], axis=1)
+        return (part + turned).reshape(n_tile, part.shape[2])
+
+    loads[3].wait()
+    loads[4].wait()
+    hidden = act.shape[1]
+    step_cols = 2 * LANES if hidden % (2 * LANES) == 0 else LANES
+    for at in range(hidden // step_cols):
+        lanes = slice(at * step_cols, (at + 1) * step_cols)
+        gate = fold(jnp.dot(x_all[...], wg[:, lanes], preferred_element_type=F32))
+        up = fold(jnp.dot(x_all[...], wu[:, lanes], preferred_element_type=F32))
+        act[:, lanes] = (gate / (1.0 + jnp.exp(-gate)) * up).astype(BF16)
+    loads[5].wait()
+    for at in range(width // wide):
+        tile = jnp.dot(act[...], wd[:, at * wide : (at + 1) * wide], preferred_element_type=F32)
+        to_blocks(back_send, at, tile)
+
+    def back_copy(target, source):
+        return remote(BACK, back_send.at[target], back_recv.at[source], target, source)
+
+    peers(lambda other: back_copy(other, me).start())
+    back_recv[me] = back_send[me]
+
+    for step in range(1, KV_HEADS):
+        other, target = column(step)
+        for copy in key_copies(other, target, head):
+            copy.wait_send()
+    for step in range(1, team):
+        for copy in team_copies(lax.rem(mate + step, team), mate):
+            copy.wait_send()
+
+    def sent(other):
+        q_copy(other, me).wait_send()
+        proj_copy(other, me).wait_send()
+        row_copy(other, me).wait_send()
+
+    peers(sent)
+    peers(lambda other: back_copy(me, other).wait_recv())
+
+    def combine(e, total):
+        block = back_recv[e].astype(F32).reshape(chunks // 2, SUB, LANES)
+        return total + mix[e][None] * block
+
+    final = lax.fori_loop(0, shards, combine, state).reshape(chunks * HALF, LANES)
+    for c in range(chunks):
+        out_ref[:, c * LANES : (c + 1) * LANES] = final[c * HALF : c * HALF + rows_dev].astype(BF16)
+    peers(lambda other: back_copy(other, me).wait_send())
+
+
+def local(*args):
+    (queries, cache_keys, _, _, _, _, residual_in, out_weight, gain, expert_gate) = args[:10]
+    shards = lax.axis_size("ctx")
+    rows_dev, width = residual_in.shape
+    capacity = max(2, 2 * rows_dev * TOP // shards)
+    if not fits(shards, rows_dev, width, capacity, expert_gate.shape[0]):
+        return plain(*args)
+    team = shards // KV_HEADS
+    hidden = expert_gate.shape[2]
+    cache = cache_keys.shape[0]
+    rows = width // LANES * HALF
+    any_spec = pl.BlockSpec(memory_space=pl.ANY)
+    vmem = pl.BlockSpec(memory_space=pltpu.VMEM)
+    smem = pl.BlockSpec(memory_space=pltpu.SMEM)
+    blocks = pltpu.VMEM((shards, rows, LANES), BF16)
+    tiles = pltpu.VMEM((team, LANES, shards * SUB), BF16)
+    stats = pltpu.VMEM((team, SUB, LANES), F32)
+    keys = pltpu.VMEM((KV_HEADS, cache, LANES), BF16)
+    new = pltpu.VMEM((KV_HEADS, 2 * SUB, LANES), BF16)
+    flops = 2 * shards * SUB * width * (3 * hidden + out_weight.shape[0])
+    return pl.pallas_call(
+        functools.partial(layer_kernel, shards),
+        out_shape=jax.ShapeDtypeStruct((rows_dev, width), BF16),
+        in_specs=[
+            vmem, any_spec, any_spec, vmem, vmem, smem, vmem,
+            any_spec, vmem, any_spec, any_spec, any_spec, vmem, vmem,
+        ],
+        out_specs=vmem,
+        scratch_shapes=[
+            pltpu.VMEM(out_weight.shape, BF16),
+            pltpu.VMEM((width, hidden), BF16),
+            pltpu.VMEM((width, hidden), BF16),
+            pltpu.VMEM((hidden, width), BF16),
+            pltpu.VMEM((KV_HEADS, team * SUB, LANES), F32),
+            pltpu.VMEM((KV_HEADS, team * SUB, LANES), BF16),
+            pltpu.VMEM((shards, team * SUB, LANES), BF16),
+            pltpu.VMEM((team, shards * SUB, LANES), BF16),
+            keys,
+            keys,
+            pltpu.VMEM((KV_HEADS, 2 * SUB, LANES), F32),
+            new,
+            new,
+            tiles,
+            tiles,
+            stats,
+            stats,
+            blocks,
+            blocks,
+            pltpu.VMEM((rows, LANES), F32),
+            pltpu.VMEM((rows, LANES), F32),
+            pltpu.VMEM((SUB, TOP), jnp.int32),
+            pltpu.VMEM((SUB, TOP), F32),
+            pltpu.VMEM((shards, SUB, LANES), F32),
+            pltpu.VMEM((rows, LANES), BF16),
+            blocks,
+            pltpu.VMEM((shards * SUB, width), BF16),
+            pltpu.VMEM((shards * SUB, hidden), BF16),
+            blocks,
+            blocks,
+            pltpu.SemaphoreType.DMA((6,)),
+            pltpu.SemaphoreType.DMA((9, shards)),
+            pltpu.SemaphoreType.DMA((9, shards)),
+        ],
+        compiler_params=pltpu.CompilerParams(
+            collective_id=0, has_side_effects=True, vmem_limit_bytes=40 * 1024 * 1024
+        ),
+        cost_estimate=pl.CostEstimate(
+            flops=flops, bytes_accessed=2 * 3 * hidden * width, transcendentals=0
+        ),
+    )(*args[:8], gain.reshape(1, -1), *args[9:])
+
+
 def solution(mesh):
     placed = (
         P(("groups", "ctx"), None),

time: 360 us -> 61.8 us (0.17)
  blocking collectives: 168 us -> 0 us
  waiting for transfers between devices: 142 us -> 0 us
  Pallas kernels: 0 us -> 46.2 us
  matrix products: 14.8 us -> 0 us
  between operations: 15 us -> 0.67 us
  other arithmetic: 10.8 us -> 0 us
  local copies, waits for them, and re-layouts: 7.41 us -> 14.2 us
    unnamed x3 -> x0, waiting for transfers between devices: 89 us -> none
    pmax x1 -> x0, blocking collectives: 57.8 us -> none  [local(): largest = lax.pmax(maxima, 'ctx')]
    psum x1 -> x0, blocking collectives: 57.6 us -> none  [local(): denoms = lax.psum(totals * rescale, 'ctx')]
    reduce_scatter x1 -> x0, waiting for transfers between devices: 53.5 us -> none  [local(): lax.psum_scatter(weighted, 'ctx', scatter_dimension=1, tiled=True)]
    pallas_call x0 -> x1, Pallas kernels: none -> 46.2 us  [local(): pl.pallas_call(functools.partial(layer_kernel, shards), out_shape=jax.Sha...]
    all_to_all x2 -> x0, blocking collectives: 26.6 us -> none  [the longest x1 13.8 us: local(): lax.all_to_all(outgoing, 'ctx', split_axis=0, concat_axis=0, tiled=True)]
    all_gather x1 -> x0, blocking collectives: 26.4 us -> none  [local(): whole_queries = lax.all_gather(queries, 'ctx', axis=0, tiled=True)]
    dot_general x7 -> x0, matrix products: 14.8 us -> none  [the longest x1 3.93 us: local(): jnp.einsum('scf,fd->scd', activated, expert_down[0], preferred_element_ty...]
  transfers between devices with their start and end apart: 2 -> 0, of which waited for: 2 -> 0; matrix products, arithmetic and copies ran while one was open for 0% -> 0% of each run, Pallas kernels for 0% -> 0%
where the time goes in v1:
time: 61.8 us; the launch traced here: 61.1 us
  Pallas kernels  46.2 us (75%)
  local copies, waits for them, and re-layouts  14.2 us (23%)
  between operations  0.67 us (1%)
    pallas_call x1, Pallas kernels, local(): pl.pallas_call(functools.partial(layer_kernel, shards), out_shape=jax.Sha...  46.2 us
    unnamed x25, local copies, waits for them, and re-layouts  13.5 us

profile of v1, /device:TPU:0, one launch (start us, length us, event | category | flops | bytes accessed | tf_op | source)
XLA Modules:
  0.0 61.1 jit_solution(1785458141432978807)
XLA Ops:
  0.7 0.7 %reshape.3.gain_ref = bf16[1,2048]{1,0:T(2,128)(2,1)S(1)} reshape(bf16[2048]{0:T(1024)(128)(2,1)} %param.22) | data formatting | bytes 8192 | tf_op jit(solution)/shard_map/reshape | solution.py:567
  1.3 0.0 copy-start
  1.3 1.9 %copy-done = bf16[1,2048,768]{2,1,0:T(8,128)(2,1)S(1)} copy-done((bf16[1,2048,768]{2,1,0:T(8,128)(2,1)S(1)}, bf16[1,2048,768]{2,1,0:T(8,128)(2,1)}, u32[]{:S(2)}) %copy-start) | copy-done | bytes 3145752
  3.2 0.0 copy-start.1
  3.2 1.9 %copy-done.1 = bf16[1,2048,768]{2,1,0:T(8,128)(2,1)S(1)} copy-done((bf16[1,2048,768]{2,1,0:T(8,128)(2,1)S(1)}, bf16[1,2048,768]{2,1,0:T(8,128)(2,1)}, u32[]{:S(2)}) %copy-start.1) | copy-done | bytes 3145752
  5.1 0.0 copy-start.2
  5.1 1.9 %copy-done.2 = bf16[1,768,2048]{2,1,0:T(8,128)(2,1)S(1)} copy-done((bf16[1,768,2048]{2,1,0:T(8,128)(2,1)S(1)}, bf16[1,768,2048]{2,1,0:T(8,128)(2,1)}, u32[]{:S(2)}) %copy-start.2) | copy-done | bytes 3145752
  7.0 0.0 copy-start.3
  7.0 1.2 %copy-done.3 = bf16[256,2048]{1,0:T(8,128)(2,1)S(1)} copy-done((bf16[256,2048]{1,0:T(8,128)(2,1)S(1)}, bf16[256,2048]{1,0:T(8,128)(2,1)}, u32[]{:S(2)}) %copy-start.3) | copy-done | bytes 1048600
  8.2 0.0 copy-start.4
  8.2 0.9 %copy-done.4 = bf16[128,512]{1,0:T(8,128)(2,1)S(1)} copy-done((bf16[128,512]{1,0:T(8,128)(2,1)S(1)}, bf16[128,512]{1,0:T(8,128)(2,1)}, u32[]{:S(2)}) %copy-start.4) | copy-done | bytes 131096
  9.1 0.0 copy-start.5
  9.1 0.9 %copy-done.5 = bf16[128,512]{1,0:T(8,128)(2,1)S(1)} copy-done((bf16[128,512]{1,0:T(8,128)(2,1)S(1)}, bf16[128,512]{1,0:T(8,128)(2,1)}, u32[]{:S(2)}) %copy-start.5) | copy-done | bytes 131096
  10.1 0.0 copy-start.6
  10.1 0.8 %copy-done.6 = bf16[3,4096]{1,0:T(4,128)(2,1)S(1)} copy-done((bf16[3,4096]{1,0:T(4,128)(2,1)S(1)}, bf16[3,4096]{1,0:T(4,128)(2,1)}, u32[]{:S(2)}) %copy-start.6) | copy-done | bytes 24600
  10.8 0.0 copy-start.7
  10.8 0.7 %copy-done.7 = bf16[3,2048]{1,0:T(4,128)(2,1)S(1)} copy-done((bf16[3,2048]{1,0:T(4,128)(2,1)S(1)}, bf16[3,2048]{1,0:T(4,128)(2,1)}, u32[]{:S(2)}) %copy-start.7) | copy-done | bytes 12312
  11.5 0.0 copy-start.8
  11.5 0.7 %copy-done.8 = bf16[3,512]{1,0:T(4,128)(2,1)S(1)} copy-done((bf16[3,512]{1,0:T(4,128)(2,1)S(1)}, bf16[3,512]{1,0:T(4,128)(2,1)}, u32[]{:S(2)}) %copy-start.8) | copy-done | bytes 3096
  12.2 0.0 copy-start.9
  12.2 0.7 %copy-done.9 = bf16[3,512]{1,0:T(4,128)(2,1)S(1)} copy-done((bf16[3,512]{1,0:T(4,128)(2,1)S(1)}, bf16[3,512]{1,0:T(4,128)(2,1)}, u32[]{:S(2)}) %copy-start.9) | copy-done | bytes 3096
  12.9 0.0 copy-start.10
  12.9 0.7 %copy-done.10 = s32[3,8]{1,0:T(4,128)S(1)} copy-done((s32[3,8]{1,0:T(4,128)S(1)}, s32[3,8]{1,0:T(4,128)}, u32[]{:S(2)}) %copy-start.10) | copy-done | bytes 120
  13.6 0.0 copy-start.11
  13.6 0.7 %copy-done.11 = f32[3,8]{1,0:T(4,128)S(1)} copy-done((f32[3,8]{1,0:T(4,128)S(1)}, f32[3,8]{1,0:T(4,128)}, u32[]{:S(2)}) %copy-start.11) | copy-done | bytes 120
  14.3 46.2 %shard_map.136 = bf16[3,2048]{1,0:T(4,128)(2,1)S(1)} custom-call(bf16[3,4096]{1,0:T(4,128)(2,1)S(1)} %copy-done.6, bf16[128,512]{1,0:T(8,128)(2,1)S(1)} %copy-done.4, bf16[128,512]{1,0:T(8,128)(2,1)S(1)} %copy-done.5, bf16[3,512]{1,0:T(4,128)(2,1)S(1)} %copy-done.8, bf16[3,512]{1,0:T(4,128)(2,1)S(1)} %copy-done.9, s32[1]{0:T(128)S(6)} %copy.16.len_ref, ...), custom_call_target="tpu_custom_call" | custom-call | flops 1342177280 | bytes 9437184 | tf_op jit(solution)/shard_map/pallas_call | solution.py:518
  60.5 0.6 copy.17
Async XLA Ops:
  1.3 1.9 %copy-start = (bf16[1,2048,768]{2,1,0:T(8,128)(2,1)S(1)}, bf16[1,2048,768]{2,1,0:T(8,128)(2,1)}, u32[]{:S(2)}) copy-start(bf16[1,2048,768]{2,1,0:T(8,128)(2,1)} %wg_ref.1) | copy-start | bytes 9437188
  3.2 1.9 %copy-start.1 = (bf16[1,2048,768]{2,1,0:T(8,128)(2,1)S(1)}, bf16[1,2048,768]{2,1,0:T(8,128)(2,1)}, u32[]{:S(2)}) copy-start(bf16[1,2048,768]{2,1,0:T(8,128)(2,1)} %wu_ref.1) | copy-start | bytes 9437188
  5.1 1.9 %copy-start.2 = (bf16[1,768,2048]{2,1,0:T(8,128)(2,1)S(1)}, bf16[1,768,2048]{2,1,0:T(8,128)(2,1)}, u32[]{:S(2)}) copy-start(bf16[1,768,2048]{2,1,0:T(8,128)(2,1)} %wd_ref.1) | copy-start | bytes 9437188
  7.0 1.2 %copy-start.3 = (bf16[256,2048]{1,0:T(8,128)(2,1)S(1)}, bf16[256,2048]{1,0:T(8,128)(2,1)}, u32[]{:S(2)}) copy-start(bf16[256,2048]{1,0:T(8,128)(2,1)} %wo_ref.1) | copy-start | bytes 3145732
  8.2 0.9 %copy-start.4 = (bf16[128,512]{1,0:T(8,128)(2,1)S(1)}, bf16[128,512]{1,0:T(8,128)(2,1)}, u32[]{:S(2)}) copy-start(bf16[128,512]{1,0:T(8,128)(2,1)} %ck_ref.1) | copy-start | bytes 393220
  9.1 0.9 %copy-start.5 = (bf16[128,512]{1,0:T(8,128)(2,1)S(1)}, bf16[128,512]{1,0:T(8,128)(2,1)}, u32[]{:S(2)}) copy-start(bf16[128,512]{1,0:T(8,128)(2,1)} %cv_ref.1) | copy-start | bytes 393220
  10.1 0.8 %copy-start.6 = (bf16[3,4096]{1,0:T(4,128)(2,1)S(1)}, bf16[3,4096]{1,0:T(4,128)(2,1)}, u32[]{:S(2)}) copy-start(bf16[3,4096]{1,0:T(4,128)(2,1)} %q_ref.1) | copy-start | bytes 73732
  10.8 0.7 %copy-start.7 = (bf16[3,2048]{1,0:T(4,128)(2,1)S(1)}, bf16[3,2048]{1,0:T(4,128)(2,1)}, u32[]{:S(2)}) copy-start(bf16[3,2048]{1,0:T(4,128)(2,1)} %res_ref.1) | copy-start | bytes 36868
  11.5 0.7 %copy-start.8 = (bf16[3,512]{1,0:T(4,128)(2,1)S(1)}, bf16[3,512]{1,0:T(4,128)(2,1)}, u32[]{:S(2)}) copy-start(bf16[3,512]{1,0:T(4,128)(2,1)} %nk_ref.1) | copy-start | bytes 9220
  12.2 0.7 %copy-start.9 = (bf16[3,512]{1,0:T(4,128)(2,1)S(1)}, bf16[3,512]{1,0:T(4,128)(2,1)}, u32[]{:S(2)}) copy-start(bf16[3,512]{1,0:T(4,128)(2,1)} %nv_ref.1) | copy-start | bytes 9220
  12.9 0.7 %copy-start.10 = (s32[3,8]{1,0:T(4,128)S(1)}, s32[3,8]{1,0:T(4,128)}, u32[]{:S(2)}) copy-start(s32[3,8]{1,0:T(4,128)} %ids_ref.1) | copy-start | bytes 292
  13.6 0.7 %copy-start.11 = (f32[3,8]{1,0:T(4,128)S(1)}, f32[3,8]{1,0:T(4,128)}, u32[]{:S(2)}) copy-start(f32[3,8]{1,0:T(4,128)} %ew_ref.1) | copy-start | bytes 292

commit v2 on v1

--- a/solution.py
+++ b/solution.py
@@ -127,7 +127,6 @@
 
 LANES = 128
 SUB = 8
-HALF = SUB // 2
 MESH = pl.DeviceIdType.MESH
 F32 = jnp.float32
 BF16 = jnp.bfloat16
@@ -141,31 +140,32 @@
     pair = HEADS // KV_HEADS // team
     return (
         experts_dev == 1
+        and team == KV_HEADS
         and HEAD_DIM == LANES
         and shards * SUB == LANES
-        and rows_dev < HALF
+        and (shards * rows_dev) % (2 * SUB) == 0
         and pair * rows_dev <= SUB
         and capacity >= rows_dev
-        and width % (4 * LANES) == 0
+        and width % (2 * SUB * LANES) == 0
     )
 
 
 def layer_kernel(
     shards,
-    q_ref,
+    q_hbm,
     ck_ref,
     cv_ref,
-    nk_ref,
-    nv_ref,
+    nk_hbm,
+    nv_hbm,
     len_ref,
-    res_ref,
+    res_hbm,
     wo_ref,
-    gain_ref,
+    gain_hbm,
     wg_ref,
     wu_ref,
     wd_ref,
-    ids_ref,
-    ew_ref,
+    ids_hbm,
+    ew_hbm,
     out_ref,
     wo,
     wg,
@@ -184,12 +184,11 @@
     num_recv,
     stat_send,
     stat_recv,
+    stage,
     proj_send,
     proj_recv,
     res_wide,
     gain_wide,
-    ids_wide,
-    ew_wide,
     mix,
     row_send,
     row_recv,
@@ -197,6 +196,13 @@
     act,
     back_send,
     back_recv,
+    q_ref,
+    nk_ref,
+    nv_ref,
+    res_ref,
+    gain_ref,
+    ids_ref,
+    ew_ref,
     load_sem,
     send_sem,
     recv_sem,
@@ -204,10 +210,10 @@
     me = lax.axis_index("ctx")
     team = shards // KV_HEADS
     pair = HEADS // KV_HEADS // team
-    rows_dev, width = res_ref.shape
+    rows_dev, width = res_hbm.shape
     chunks = width // LANES
     cache = ck_ref.shape[0]
-    head, mate = me // team, me % team
+    plane, mate = me // team, me % team
 
     barrier = pltpu.get_barrier_semaphore()
 
@@ -219,17 +225,33 @@
 
     lax.fori_loop(1, shards, greet, 0)
 
-    own_lanes = pl.ds(pl.multiple_of(head * LANES, LANES), LANES)
+    own_lanes = pl.ds(pl.multiple_of(mate * LANES, LANES), LANES)
+    small = [
+        (q_hbm, q_ref),
+        (nk_hbm, nk_ref),
+        (nv_hbm, nv_ref),
+        (res_hbm, res_ref),
+        (gain_hbm, gain_ref),
+        (ids_hbm, ids_ref),
+        (ew_hbm, ew_ref),
+    ]
+    large = [
+        (ck_ref.at[:, own_lanes], k_all.at[mate]),
+        (cv_ref.at[:, own_lanes], v_all.at[mate]),
+        (wo_ref, wo),
+        (wg_ref.at[0], wg),
+        (wu_ref.at[0], wu),
+        (wd_ref.at[0], wd),
+    ]
     loads = [
-        pltpu.make_async_copy(ck_ref.at[:, own_lanes], k_all.at[head], load_sem.at[0]),
-        pltpu.make_async_copy(cv_ref.at[:, own_lanes], v_all.at[head], load_sem.at[1]),
-        pltpu.make_async_copy(wo_ref, wo, load_sem.at[2]),
-        pltpu.make_async_copy(wg_ref.at[0], wg, load_sem.at[3]),
-        pltpu.make_async_copy(wu_ref.at[0], wu, load_sem.at[4]),
-        pltpu.make_async_copy(wd_ref.at[0], wd, load_sem.at[5]),
+        pltpu.make_async_copy(src, dst, load_sem.at[i])
+        for i, (src, dst) in enumerate(small + large)
     ]
     for load in loads:
         load.start()
+    for load in loads[: len(small)]:
+        load.wait()
+    loads = loads[len(small) :]
 
     q_wide[...] = jnp.zeros_like(q_wide)
     for one in range(HEADS):
@@ -258,17 +280,17 @@
             device_id_type=MESH,
         )
 
-    def column(step):
-        other = lax.rem(head + step, KV_HEADS)
-        return other, other * team + mate
-
-    def key_copies(other, target, source_head):
-        lanes = pl.ds(pl.multiple_of(other * LANES, LANES), LANES)
-        source = source_head * team + mate
+    def near(step):
+        other = lax.rem(mate + step, team)
+        return other, plane * team + other
+
+    def key_copies(lane_head, target, source_mate):
+        lanes = pl.ds(pl.multiple_of(lane_head * LANES, LANES), LANES)
+        source = plane * team + source_mate
         return (
-            remote(K, ck_ref.at[:, lanes], k_all.at[source_head], target, source),
-            remote(V, cv_ref.at[:, lanes], v_all.at[source_head], target, source),
-            remote(NEW, new_send.at[other], new_recv.at[source_head], target, source),
+            remote(K, ck_ref.at[:, lanes], k_all.at[source_mate], target, source),
+            remote(V, cv_ref.at[:, lanes], v_all.at[source_mate], target, source),
+            remote(NEW, new_send.at[lane_head], new_recv.at[source_mate], target, source),
         )
 
     pl.semaphore_wait(barrier, shards - 1)
@@ -281,32 +303,25 @@
         lax.fori_loop(1, shards, step_body, 0)
 
     def q_copy(target, source):
-        return remote(Q, q_send.at[target // team], q_recv.at[source], target, source)
-
-    for step in range(1, KV_HEADS):
-        for copy in key_copies(*column(step), head):
+        return remote(Q, q_send.at[target % team], q_recv.at[source], target, source)
+
+    peers(lambda other: q_copy(other, me).start())
+    for step in range(1, team):
+        for copy in key_copies(*near(step), mate):
             copy.start()
-    peers(lambda other: q_copy(other, me).start())
-
-    q_recv[me] = q_send[head]
-    new_recv[head] = new_send[head]
-
-    res_wide[...] = jnp.zeros_like(res_wide)
+
+    q_recv[me] = q_send[mate]
+    new_recv[mate] = new_send[mate]
+
     for c in range(chunks):
         lanes = slice(c * LANES, (c + 1) * LANES)
-        res_wide[c * HALF : c * HALF + rows_dev, :] = res_ref[:, lanes].astype(F32)
-        gain_wide[c * HALF : (c + 1) * HALF, :] = jnp.broadcast_to(
-            gain_ref[:, lanes].astype(F32), (HALF, LANES)
-        )
-    ids_wide[...] = jnp.full_like(ids_wide, -1)
-    ew_wide[...] = jnp.zeros_like(ew_wide)
-    for half in range(2):
-        at = slice(half * HALF, half * HALF + rows_dev)
-        ids_wide[at, :] = ids_ref[...]
-        ew_wide[at, :] = ew_ref[...]
+        res_wide[pl.ds(c, rows_dev, stride=chunks), :] = res_ref[:, lanes].astype(F32)
+        gain_wide[c : c + 1, :] = gain_ref[lanes].astype(F32).reshape(1, LANES)
     for e in range(shards):
-        share = jnp.where(ids_wide[...] == e, ew_wide[...], 0.0)
-        mix[e] = jnp.broadcast_to(jnp.sum(share, axis=1, keepdims=True), (SUB, LANES))
+        share = jnp.where(ids_ref[...] == e, ew_ref[...], 0.0)
+        mix[e, 0:rows_dev, :] = jnp.broadcast_to(
+            jnp.sum(share, axis=1, keepdims=True), (rows_dev, LANES)
+        )
 
     peers(lambda other: q_copy(me, other).wait_recv())
     gathered = q_recv[...].astype(F32).reshape(shards, team, SUB, LANES)
@@ -314,39 +329,38 @@
         q_heads[one] = gathered[:, one].reshape(shards * SUB, LANES).astype(BF16)
     loads[0].wait()
     loads[1].wait()
-    for step in range(1, KV_HEADS):
-        other, _ = column(step)
-        for copy in key_copies(head, me, other):
+    for step in range(1, team):
+        other, _ = near(step)
+        for copy in key_copies(mate, me, other):
             copy.wait_recv()
 
-    n_cache = KV_HEADS * cache
-    n_new = KV_HEADS * SUB
+    n_cache = team * cache
+    n_new = team * SUB
     fresh = new_recv[...].astype(F32)
     new_k = fresh[:, 0:SUB].reshape(n_new, LANES).astype(BF16)
     new_v = fresh[:, SUB : 2 * SUB].reshape(n_new, LANES).astype(BF16)
     lengths = fresh[:, rows_dev : rows_dev + 1, :]
-    spot = lax.broadcasted_iota(jnp.int32, (KV_HEADS, cache, LANES), 1).astype(F32)
+    spot = lax.broadcasted_iota(jnp.int32, (team, cache, LANES), 1).astype(F32)
     cache_ok = (spot < lengths).reshape(n_cache, LANES)
     lane = lax.broadcasted_iota(jnp.int32, (n_new, LANES), 1)
     place = lax.broadcasted_iota(jnp.int32, (n_new, LANES), 0)
     row_of = (lane // SUB) * rows_dev + (lane % SUB) % rows_dev
     key_at = place % SUB
-    span = ((place // SUB) * team + mate) * rows_dev + key_at
+    span = (plane * team + place // SUB) * rows_dev + key_at
     new_ok = (key_at < rows_dev) & (span <= row_of)
     across = (((1,), (1,)), ((), ()))
     down = (((0,), (0,)), ((), ()))
     scale = HEAD_DIM ** (-0.5)
     stat_row = lax.broadcasted_iota(jnp.int32, (SUB, LANES), 0)
 
-    def team_copies(target_mate, source_mate):
-        target, source = head * team + target_mate, head * team + source_mate
+    def head_copies(target, target_mate, source, source_plane):
         return (
-            remote(NUM, num_send.at[target_mate], num_recv.at[source_mate], target, source),
-            remote(STAT, stat_send.at[target_mate], stat_recv.at[source_mate], target, source),
+            remote(NUM, num_send.at[target_mate], num_recv.at[source_plane], target, source),
+            remote(STAT, stat_send.at[target_mate], stat_recv.at[source_plane], target, source),
         )
 
     def attend(step, carry):
-        to = lax.rem(mate + step, team)
+        to = lax.rem(plane + step, team)
         queries = q_heads[to]
         keys = k_all[...].reshape(n_cache, LANES)
         old = lax.dot_general(keys, queries, across, preferred_element_type=F32) * scale
@@ -365,35 +379,41 @@
         num_send[to] = numer.astype(BF16)
         stat_send[to] = jnp.where(stat_row == 0, top, total)
 
-        @pl.when(step < team)
+        target = mate * team + to
+
+        @pl.when(target != me)
         def _():
-            for copy in team_copies(to, mate):
+            for copy in head_copies(target, to, me, plane):
                 copy.start()
 
+        @pl.when(target == me)
+        def _():
+            num_recv[plane] = num_send[to]
+            stat_recv[plane] = stat_send[to]
+
         return carry
 
-    lax.fori_loop(1, team + 1, attend, 0)
-    num_recv[mate] = num_send[mate]
-    stat_recv[mate] = stat_send[mate]
-    for step in range(1, team):
-        for copy in team_copies(mate, lax.rem(mate + step, team)):
-            copy.wait_recv()
+    lax.fori_loop(0, team, attend, 0)
+    for at in range(team):
+        source = at * team + plane
+
+        @pl.when(source != me)
+        def _():
+            for copy in head_copies(me, mate, source, at):
+                copy.wait_recv()
+
     tops = stat_recv[:, 0:1, :]
     weight = jnp.exp(tops - jnp.max(tops, axis=0, keepdims=True))
     weight = weight / jnp.sum(weight * stat_recv[:, 1:2, :], axis=0, keepdims=True)
     attention = jnp.sum(num_recv[...].astype(F32) * weight, axis=0).astype(BF16)
 
-    n_tile = shards * SUB
-    tile_row = lax.broadcasted_iota(jnp.int32, (n_tile, LANES), 0)
-    tile_lane = lax.broadcasted_iota(jnp.int32, (n_tile, LANES), 1)
-    odd = (tile_row % SUB) >= HALF
-    own_row = tile_row % HALF
+    n_rows = shards * rows_dev
+    tile_row = lax.broadcasted_iota(jnp.int32, (n_rows, LANES), 0)
+    tile_lane = lax.broadcasted_iota(jnp.int32, (n_rows, LANES), 1)
     parts = []
     for which in range(pair):
-        pick = (
-            (tile_row // SUB == tile_lane // SUB)
-            & (own_row < rows_dev)
-            & (tile_lane % SUB == which * rows_dev + own_row)
+        pick = (tile_row // rows_dev == tile_lane // SUB) & (
+            tile_lane % SUB == which * rows_dev + tile_row % rows_dev
         )
         pick = jnp.where(pick, 1.0, 0.0).astype(BF16)
         parts.append(
@@ -401,19 +421,18 @@
         )
     columns = jnp.concatenate(parts, axis=1)
 
-    def to_blocks(ref, at, tile):
-        pieces = []
-        for j in range(2):
-            left = tile[:, 2 * j * LANES : (2 * j + 1) * LANES]
-            right = tile[:, (2 * j + 1) * LANES : (2 * j + 2) * LANES]
-            pieces.append(jnp.where(odd, right, left).reshape(shards, SUB, LANES))
-        ref[:, at * 2 * SUB : (at + 1) * 2 * SUB, :] = jnp.concatenate(pieces, axis=1).astype(BF16)
+    def spread(first, tile):
+        for j in range(tile.shape[1] // LANES):
+            stage[pl.ds(first + j, n_rows, stride=chunks), :] = tile[
+                :, j * LANES : (j + 1) * LANES
+            ]
 
     loads[2].wait()
     wide = 4 * LANES
     for at in range(width // wide):
         tile = jnp.dot(columns, wo[:, at * wide : (at + 1) * wide], preferred_element_type=F32)
-        to_blocks(proj_send, at, tile)
+        spread(4 * at, tile)
+    proj_send[...] = stage[...].reshape(proj_send.shape).astype(BF16)
 
     def proj_copy(target, source):
         return remote(PROJ, proj_send.at[target], proj_recv.at[source], target, source)
@@ -422,11 +441,10 @@
     proj_recv[me] = proj_send[me]
     peers(lambda other: proj_copy(me, other).wait_recv())
     state = res_wide[...] + jnp.sum(proj_recv[...].astype(F32), axis=0)
-    state = state.reshape(chunks // 2, SUB, LANES)
-    squares = jnp.sum(jnp.sum(state * state, axis=0), axis=1, keepdims=True)
-    squares = squares + jnp.concatenate([squares[HALF:], squares[:HALF]], axis=0)
-    normed = state * lax.rsqrt(squares / width + epsilon)[None]
-    normed = normed.reshape(chunks * HALF, LANES) * gain_wide[...]
+    state = state.reshape(rows_dev, chunks, LANES)
+    squares = jnp.sum(jnp.sum(state * state, axis=1, keepdims=True), axis=2, keepdims=True)
+    normed = state * lax.rsqrt(squares / width + epsilon) * gain_wide[...][None]
+    normed = normed.reshape(rows_dev * chunks, LANES)
     row_send[...] = normed.astype(BF16)
 
     def row_copy(target, source):
@@ -436,18 +454,11 @@
     row_recv[me] = row_send[...]
     peers(lambda other: row_copy(me, other).wait_recv())
 
-    for at in range(chunks // 4):
-        both = row_recv[:, at * 2 * SUB : (at + 1) * 2 * SUB, :].astype(F32)
-        for j in range(2):
-            piece = both[:, j * SUB : (j + 1) * SUB].reshape(n_tile, LANES)
-            start = (4 * at + 2 * j) * LANES
-            x_all[:, start : start + LANES] = jnp.where(odd, 0.0, piece).astype(BF16)
-            x_all[:, start + LANES : start + 2 * LANES] = jnp.where(odd, piece, 0.0).astype(BF16)
-
-    def fold(part):
-        part = part.reshape(shards, SUB, part.shape[1])
-        turned = jnp.concatenate([part[:, HALF:], part[:, :HALF]], axis=1)
-        return (part + turned).reshape(n_tile, part.shape[2])
+    stage[...] = row_recv[...].astype(F32).reshape(stage.shape)
+    for c in range(chunks):
+        x_all[:, c * LANES : (c + 1) * LANES] = stage[
+            pl.ds(c, n_rows, stride=chunks), :
+        ].astype(BF16)
 
     loads[3].wait()
     loads[4].wait()
@@ -455,13 +466,14 @@
     step_cols = 2 * LANES if hidden % (2 * LANES) == 0 else LANES
     for at in range(hidden // step_cols):
         lanes = slice(at * step_cols, (at + 1) * step_cols)
-        gate = fold(jnp.dot(x_all[...], wg[:, lanes], preferred_element_type=F32))
-        up = fold(jnp.dot(x_all[...], wu[:, lanes], preferred_element_type=F32))
+        gate = jnp.dot(x_all[...], wg[:, lanes], preferred_element_type=F32)
+        up = jnp.dot(x_all[...], wu[:, lanes], preferred_element_type=F32)
         act[:, lanes] = (gate / (1.0 + jnp.exp(-gate)) * up).astype(BF16)
     loads[5].wait()
     for at in range(width // wide):
         tile = jnp.dot(act[...], wd[:, at * wide : (at + 1) * wide], preferred_element_type=F32)
-        to_blocks(back_send, at, tile)
+        spread(4 * at, tile)
+    back_send[...] = stage[...].reshape(back_send.shape).astype(BF16)
 
     def back_copy(target, source):
         return remote(BACK, back_send.at[target], back_recv.at[source], target, source)
@@ -469,13 +481,16 @@
     peers(lambda other: back_copy(other, me).start())
     back_recv[me] = back_send[me]
 
-    for step in range(1, KV_HEADS):
-        other, target = column(step)
-        for copy in key_copies(other, target, head):
+    for step in range(1, team):
+        for copy in key_copies(*near(step), mate):
             copy.wait_send()
-    for step in range(1, team):
-        for copy in team_copies(lax.rem(mate + step, team), mate):
-            copy.wait_send()
+    for at in range(team):
+        target = mate * team + at
+
+        @pl.when(target != me)
+        def _():
+            for copy in head_copies(target, at, me, plane):
+                copy.wait_send()
 
     def sent(other):
         q_copy(other, me).wait_send()
@@ -486,17 +501,22 @@
     peers(lambda other: back_copy(me, other).wait_recv())
 
     def combine(e, total):
-        block = back_recv[e].astype(F32).reshape(chunks // 2, SUB, LANES)
-        return total + mix[e][None] * block
-
-    final = lax.fori_loop(0, shards, combine, state).reshape(chunks * HALF, LANES)
+        block = back_recv[e].astype(F32).reshape(rows_dev, chunks, LANES)
+        share = mix[e]
+        return tuple(total[r] + share[r : r + 1, :] * block[r] for r in range(rows_dev))
+
+    final = lax.fori_loop(0, shards, combine, tuple(state[r] for r in range(rows_dev)))
+    for r in range(rows_dev):
+        res_wide[r * chunks : (r + 1) * chunks, :] = final[r]
     for c in range(chunks):
-        out_ref[:, c * LANES : (c + 1) * LANES] = final[c * HALF : c * HALF + rows_dev].astype(BF16)
+        out_ref[:, c * LANES : (c + 1) * LANES] = res_wide[
+            pl.ds(c, rows_dev, stride=chunks), :
+        ].astype(BF16)
     peers(lambda other: back_copy(other, me).wait_send())
 
 
 def local(*args):
-    (queries, cache_keys, _, _, _, _, residual_in, out_weight, gain, expert_gate) = args[:10]
+    (queries, cache_keys, _, _, _, _, residual_in, out_weight, _, expert_gate) = args[:10]
     shards = lax.axis_size("ctx")
     rows_dev, width = residual_in.shape
     capacity = max(2, 2 * rows_dev * TOP // shards)
@@ -505,23 +525,20 @@
     team = shards // KV_HEADS
     hidden = expert_gate.shape[2]
     cache = cache_keys.shape[0]
-    rows = width // LANES * HALF
+    rows = rows_dev * width // LANES
     any_spec = pl.BlockSpec(memory_space=pl.ANY)
     vmem = pl.BlockSpec(memory_space=pltpu.VMEM)
     smem = pl.BlockSpec(memory_space=pltpu.SMEM)
     blocks = pltpu.VMEM((shards, rows, LANES), BF16)
     tiles = pltpu.VMEM((team, LANES, shards * SUB), BF16)
     stats = pltpu.VMEM((team, SUB, LANES), F32)
-    keys = pltpu.VMEM((KV_HEADS, cache, LANES), BF16)
+    keys = pltpu.VMEM((team, cache, LANES), BF16)
     new = pltpu.VMEM((KV_HEADS, 2 * SUB, LANES), BF16)
-    flops = 2 * shards * SUB * width * (3 * hidden + out_weight.shape[0])
+    flops = 2 * shards * rows_dev * width * (3 * hidden + out_weight.shape[0])
     return pl.pallas_call(
         functools.partial(layer_kernel, shards),
         out_shape=jax.ShapeDtypeStruct((rows_dev, width), BF16),
-        in_specs=[
-            vmem, any_spec, any_spec, vmem, vmem, smem, vmem,
-            any_spec, vmem, any_spec, any_spec, any_spec, vmem, vmem,
-        ],
+        in_specs=[any_spec] * 5 + [smem] + [any_spec] * 8,
         out_specs=vmem,
         scratch_shapes=[
             pltpu.VMEM(out_weight.shape, BF16),
@@ -541,30 +558,32 @@
             tiles,
             stats,
             stats,
+            pltpu.VMEM((shards * rows, LANES), F32),
             blocks,
             blocks,
             pltpu.VMEM((rows, LANES), F32),
-            pltpu.VMEM((rows, LANES), F32),
-            pltpu.VMEM((SUB, TOP), jnp.int32),
-            pltpu.VMEM((SUB, TOP), F32),
+            pltpu.VMEM((width // LANES, LANES), F32),
             pltpu.VMEM((shards, SUB, LANES), F32),
             pltpu.VMEM((rows, LANES), BF16),
             blocks,
-            pltpu.VMEM((shards * SUB, width), BF16),
-            pltpu.VMEM((shards * SUB, hidden), BF16),
+            pltpu.VMEM((shards * rows_dev, width), BF16),
+            pltpu.VMEM((shards * rows_dev, hidden), BF16),
             blocks,
             blocks,
-            pltpu.SemaphoreType.DMA((6,)),
+            *(pltpu.VMEM(args[i].shape, args[i].dtype) for i in (0, 3, 4, 6)),
+            pltpu.VMEM((width,), BF16),
+            *(pltpu.VMEM(args[i].shape, args[i].dtype) for i in (12, 13)),
+            pltpu.SemaphoreType.DMA((13,)),
             pltpu.SemaphoreType.DMA((9, shards)),
             pltpu.SemaphoreType.DMA((9, shards)),
         ],
         compiler_params=pltpu.CompilerParams(
-            collective_id=0, has_side_effects=True, vmem_limit_bytes=40 * 1024 * 1024
+            collective_id=0, has_side_effects=True, vmem_limit_bytes=60 * 1024 * 1024
         ),
         cost_estimate=pl.CostEstimate(
             flops=flops, bytes_accessed=2 * 3 * hidden * width, transcendentals=0
         ),
-    )(*args[:8], gain.reshape(1, -1), *args[9:])
+    )(*args)
 
 
 def solution(mesh):

time: 61.8 us -> 45.2 us (0.73)
  local copies, waits for them, and re-layouts: 14.2 us -> 1.33 us
  Pallas kernels: 46.2 us -> 42.9 us
    unnamed x25 -> x1, local copies, waits for them, and re-layouts: 13.5 us -> 1.33 us
    pallas_call x1, Pallas kernels: 46.2 us -> 42.9 us  [local(): pl.pallas_call(functools.partial(layer_kernel, shards), out_shape=jax.Sha...]
    reshape x1 -> x0, local copies, waits for them, and re-layouts: 0.69 us -> none  [local(): gain.reshape(1, -1)]
where the time goes in v2:
time: 45.2 us; the launch traced here: 44.9 us
  Pallas kernels  42.9 us (95%)
  local copies, waits for them, and re-layouts  1.33 us (3%)
  between operations  0.66 us (1%)
    pallas_call x1, Pallas kernels, local(): pl.pallas_call(functools.partial(layer_kernel, shards), out_shape=jax.Sha...  42.9 us
    unnamed x1, local copies, waits for them, and re-layouts  1.33 us

profile of v2, /device:TPU:0, one launch (start us, length us, event | category | flops | bytes accessed | tf_op | source)
XLA Modules:
  0.0 44.9 jit_solution(18205620225952388461)
XLA Ops:
  0.7 42.9 %shard_map.136 = bf16[3,2048]{1,0:T(4,128)(2,1)} custom-call(bf16[3,4096]{1,0:T(4,128)(2,1)} %q_hbm.1, bf16[128,512]{1,0:T(8,128)(2,1)} %ck_ref.1, bf16[128,512]{1,0:T(8,128)(2,1)} %cv_ref.1, bf16[3,512]{1,0:T(4,128)(2,1)} %nk_hbm.1, bf16[3,512]{1,0:T(4,128)(2,1)} %nv_hbm.1, s32[1]{0:T(128)S(6)} %copy.16.len_ref, bf16[3,2048]{1,0:T(4,128)(2,1)} %res_hbm.1, ...), custom_call_target="tpu_custom_call" | custom-call | flops 503316480 | bytes 9437184 | tf_op jit(solution)/shard_map/pallas_call | solution.py:538
  43.6 1.3 %copy.17 = bf16[3,2048]{1,0:T(4,128)(2,1)} copy(bf16[3,2048]{1,0:T(4,128)(2,1)} %shard_map.136) | data formatting | bytes 24576

commit v3 on v2

--- a/solution.py
+++ b/solution.py
@@ -130,7 +130,8 @@
 MESH = pl.DeviceIdType.MESH
 F32 = jnp.float32
 BF16 = jnp.bfloat16
-Q, K, V, NEW, NUM, STAT, PROJ, ROWS, BACK = range(9)
+Q, K, V, NEW, NUM, STAT, PROJ, ROWS, BACK, PROJ_PAIR, ROWS_PAIR, BACK_PAIR = range(12)
+KINDS = 12
 
 
 def fits(shards, rows_dev, width, capacity, experts_dev):
@@ -144,7 +145,9 @@
         and HEAD_DIM == LANES
         and shards * SUB == LANES
         and (shards * rows_dev) % (2 * SUB) == 0
-        and pair * rows_dev <= SUB
+        and pair * rows_dev <= SUB - 2
+        and rows_dev <= team
+        and shards <= LANES
         and capacity >= rows_dev
         and width % (2 * SUB * LANES) == 0
     )
@@ -185,15 +188,20 @@
     stat_send,
     stat_recv,
     stage,
+    proj_away,
+    proj_near,
     proj_send,
     proj_recv,
     res_wide,
     gain_wide,
+    mix_all,
     mix,
     row_send,
     row_recv,
     x_all,
     act,
+    back_away,
+    back_near,
     back_send,
     back_recv,
     q_ref,
@@ -214,6 +222,9 @@
     chunks = width // LANES
     cache = ck_ref.shape[0]
     plane, mate = me // team, me % team
+    chips = shards // 2
+    chip, core = me // 2, me % 2
+    sibling = me + 1 - 2 * core
 
     barrier = pltpu.get_barrier_semaphore()
 
@@ -247,11 +258,11 @@
         pltpu.make_async_copy(src, dst, load_sem.at[i])
         for i, (src, dst) in enumerate(small + large)
     ]
-    for load in loads:
+    early = len(small) + 2
+    for load in loads[:early]:
         load.start()
     for load in loads[: len(small)]:
         load.wait()
-    loads = loads[len(small) :]
 
     q_wide[...] = jnp.zeros_like(q_wide)
     for one in range(HEADS):
@@ -260,6 +271,16 @@
         q_wide[kv, pl.ds(who * SUB + which * rows_dev, rows_dev), :] = q_ref[
             :, one * LANES : (one + 1) * LANES
         ].astype(F32)
+    expert = lax.broadcasted_iota(jnp.int32, (rows_dev, LANES), 1)
+    routed = jnp.zeros((rows_dev, LANES), F32)
+    for k in range(TOP):
+        routed += jnp.where(expert == ids_ref[:, k : k + 1], ew_ref[:, k : k + 1], 0.0)
+    coarse = routed.astype(BF16).astype(F32)
+    fine = routed - coarse
+    for kv in range(KV_HEADS):
+        for r in range(rows_dev):
+            q_wide[kv, (r + 1) * SUB - 2 : (r + 1) * SUB - 1, :] = coarse[r : r + 1]
+            q_wide[kv, (r + 1) * SUB - 1 : (r + 1) * SUB, :] = fine[r : r + 1]
     q_send[...] = q_wide[...].astype(BF16)
     new_wide[...] = jnp.zeros_like(new_wide)
     live = jnp.full((1, LANES), len_ref[0], jnp.int32).astype(F32)
@@ -309,6 +330,9 @@
     for step in range(1, team):
         for copy in key_copies(*near(step), mate):
             copy.start()
+    for load in loads[early:]:
+        load.start()
+    loads = loads[len(small) :]
 
     q_recv[me] = q_send[mate]
     new_recv[mate] = new_send[mate]
@@ -317,16 +341,20 @@
         lanes = slice(c * LANES, (c + 1) * LANES)
         res_wide[pl.ds(c, rows_dev, stride=chunks), :] = res_ref[:, lanes].astype(F32)
         gain_wide[c : c + 1, :] = gain_ref[lanes].astype(F32).reshape(1, LANES)
-    for e in range(shards):
-        share = jnp.where(ids_ref[...] == e, ew_ref[...], 0.0)
-        mix[e, 0:rows_dev, :] = jnp.broadcast_to(
-            jnp.sum(share, axis=1, keepdims=True), (rows_dev, LANES)
-        )
 
     peers(lambda other: q_copy(me, other).wait_recv())
     gathered = q_recv[...].astype(F32).reshape(shards, team, SUB, LANES)
     for one in range(team):
         q_heads[one] = gathered[:, one].reshape(shards * SUB, LANES).astype(BF16)
+    at_lane = lax.broadcasted_iota(jnp.int32, (shards, LANES), 1)
+    for r in range(rows_dev):
+        both = gathered[:, r, SUB - 2, :] + gathered[:, r, SUB - 1, :]
+        mine = jnp.sum(jnp.where(at_lane == me, both, 0.0), axis=1, keepdims=True)
+        mix_all[...] = jnp.broadcast_to(mine, (shards, LANES))
+        for half in range(2):
+            mix[pl.ds(half * chips * rows_dev + r, chips, stride=rows_dev), :] = mix_all[
+                pl.ds(half, chips, stride=2), :
+            ]
     loads[0].wait()
     loads[1].wait()
     for step in range(1, team):
@@ -410,9 +438,11 @@
     n_rows = shards * rows_dev
     tile_row = lax.broadcasted_iota(jnp.int32, (n_rows, LANES), 0)
     tile_lane = lax.broadcasted_iota(jnp.int32, (n_rows, LANES), 1)
+    tile_place = tile_row // rows_dev
+    tile_device = (tile_place % chips) * 2 + tile_place // chips
     parts = []
     for which in range(pair):
-        pick = (tile_row // rows_dev == tile_lane // SUB) & (
+        pick = (tile_device == tile_lane // SUB) & (
             tile_lane % SUB == which * rows_dev + tile_row % rows_dev
         )
         pick = jnp.where(pick, 1.0, 0.0).astype(BF16)
@@ -432,14 +462,47 @@
     for at in range(width // wide):
         tile = jnp.dot(columns, wo[:, at * wide : (at + 1) * wide], preferred_element_type=F32)
         spread(4 * at, tile)
-    proj_send[...] = stage[...].reshape(proj_send.shape).astype(BF16)
-
-    def proj_copy(target, source):
-        return remote(PROJ, proj_send.at[target], proj_recv.at[source], target, source)
-
-    peers(lambda other: proj_copy(other, me).start())
-    proj_recv[me] = proj_send[me]
-    peers(lambda other: proj_copy(me, other).wait_recv())
+
+    half_rows = chips * rows_dev * chunks
+    own_half = pl.ds(pl.multiple_of(core * half_rows, half_rows), half_rows)
+    away_half = pl.ds(pl.multiple_of((1 - core) * half_rows, half_rows), half_rows)
+
+    def others(body):
+        def step_body(step, carry):
+            body(lax.rem(chip + step, chips))
+            return carry
+
+        lax.fori_loop(1, chips, step_body, 0)
+
+    def reduce_copies(pair_kind, kind, away, near, send, recv):
+        def pair_copy(target, source):
+            return remote(pair_kind, away, near, target, source)
+
+        def copy(target_chip, source_chip):
+            return remote(
+                kind,
+                send.at[target_chip],
+                recv.at[source_chip],
+                target_chip * 2 + core,
+                source_chip * 2 + core,
+            )
+
+        return pair_copy, copy
+
+    def reduce_to_owners(copies, away, near, send, recv):
+        pair_copy, copy = copies
+        away[...] = stage[away_half, :].astype(BF16).reshape(away.shape)
+        pair_copy(sibling, me).start()
+        pair_copy(me, sibling).wait_recv()
+        total = stage[own_half, :].reshape(near.shape) + near[...].astype(F32)
+        send[...] = total.astype(BF16)
+        others(lambda other: copy(other, chip).start())
+        recv[chip] = send[chip]
+
+    proj_refs = (proj_away, proj_near, proj_send, proj_recv)
+    proj_copies = reduce_copies(PROJ_PAIR, PROJ, *proj_refs)
+    reduce_to_owners(proj_copies, *proj_refs)
+    others(lambda other: proj_copies[1](chip, other).wait_recv())
     state = res_wide[...] + jnp.sum(proj_recv[...].astype(F32), axis=0)
     state = state.reshape(rows_dev, chunks, LANES)
     squares = jnp.sum(jnp.sum(state * state, axis=1, keepdims=True), axis=2, keepdims=True)
@@ -447,13 +510,36 @@
     normed = normed.reshape(rows_dev * chunks, LANES)
     row_send[...] = normed.astype(BF16)
 
-    def row_copy(target, source):
-        return remote(ROWS, row_send, row_recv.at[source], target, source)
-
-    peers(lambda other: row_copy(other, me).start())
-    row_recv[me] = row_send[...]
-    peers(lambda other: row_copy(me, other).wait_recv())
-
+    def row_copy(target, source_chip):
+        source = source_chip * 2 + core
+        return remote(ROWS, row_send, row_recv.at[core * chips + source_chip], target, source)
+
+    def row_pair_copy(target, source, at):
+        block = row_recv.at[at]
+        return pltpu.make_async_remote_copy(
+            src_ref=block,
+            dst_ref=block,
+            send_sem=send_sem.at[ROWS_PAIR, at],
+            recv_sem=recv_sem.at[ROWS_PAIR, at],
+            device_id={"ctx": target},
+            device_id_type=MESH,
+        )
+
+    others(lambda other: row_copy(other * 2 + core, chip).start())
+    row_recv[core * chips + chip] = row_send[...]
+    row_pair_copy(sibling, me, core * chips + chip).start()
+
+    def hand_on(other):
+        row_copy(me, other).wait_recv()
+        row_pair_copy(sibling, me, core * chips + other).start()
+
+    others(hand_on)
+
+    def handed(at, carry):
+        row_pair_copy(me, sibling, (1 - core) * chips + at).wait_recv()
+        return carry
+
+    lax.fori_loop(0, chips, handed, 0)
     stage[...] = row_recv[...].astype(F32).reshape(stage.shape)
     for c in range(chunks):
         x_all[:, c * LANES : (c + 1) * LANES] = stage[
@@ -472,14 +558,10 @@
     loads[5].wait()
     for at in range(width // wide):
         tile = jnp.dot(act[...], wd[:, at * wide : (at + 1) * wide], preferred_element_type=F32)
-        spread(4 * at, tile)
-    back_send[...] = stage[...].reshape(back_send.shape).astype(BF16)
-
-    def back_copy(target, source):
-        return remote(BACK, back_send.at[target], back_recv.at[source], target, source)
-
-    peers(lambda other: back_copy(other, me).start())
-    back_recv[me] = back_send[me]
+        spread(4 * at, tile * jnp.concatenate([mix[...]] * 4, axis=1))
+    back_refs = (back_away, back_near, back_send, back_recv)
+    back_copies = reduce_copies(BACK_PAIR, BACK, *back_refs)
+    reduce_to_owners(back_copies, *back_refs)
 
     for step in range(1, team):
         for copy in key_copies(*near(step), mate):
@@ -492,27 +574,26 @@
             for copy in head_copies(target, at, me, plane):
                 copy.wait_send()
 
+    peers(lambda other: q_copy(other, me).wait_send())
+    proj_copies[0](sibling, me).wait_send()
+    back_copies[0](sibling, me).wait_send()
+
     def sent(other):
-        q_copy(other, me).wait_send()
-        proj_copy(other, me).wait_send()
-        row_copy(other, me).wait_send()
-
-    peers(sent)
-    peers(lambda other: back_copy(me, other).wait_recv())
-
-    def combine(e, total):
-        block = back_recv[e].astype(F32).reshape(rows_dev, chunks, LANES)
-        share = mix[e]
-        return tuple(total[r] + share[r : r + 1, :] * block[r] for r in range(rows_dev))
-
-    final = lax.fori_loop(0, shards, combine, tuple(state[r] for r in range(rows_dev)))
+        proj_copies[1](other, chip).wait_send()
+        row_copy(other * 2 + core, chip).wait_send()
+        row_pair_copy(sibling, me, core * chips + other).wait_send()
+
+    others(sent)
+    row_pair_copy(sibling, me, core * chips + chip).wait_send()
+    others(lambda other: back_copies[1](chip, other).wait_recv())
+    final = state + jnp.sum(back_recv[...].astype(F32), axis=0).reshape(state.shape)
     for r in range(rows_dev):
         res_wide[r * chunks : (r + 1) * chunks, :] = final[r]
     for c in range(chunks):
         out_ref[:, c * LANES : (c + 1) * LANES] = res_wide[
             pl.ds(c, rows_dev, stride=chunks), :
         ].astype(BF16)
-    peers(lambda other: back_copy(other, me).wait_send())
+    others(lambda other: back_copies[1](other, chip).wait_send())
 
 
 def local(*args):
@@ -530,6 +611,7 @@
     vmem = pl.BlockSpec(memory_space=pltpu.VMEM)
     smem = pl.BlockSpec(memory_space=pltpu.SMEM)
     blocks = pltpu.VMEM((shards, rows, LANES), BF16)
+    halves = pltpu.VMEM((shards // 2, rows, LANES), BF16)
     tiles = pltpu.VMEM((team, LANES, shards * SUB), BF16)
     stats = pltpu.VMEM((team, SUB, LANES), F32)
     keys = pltpu.VMEM((team, cache, LANES), BF16)
@@ -559,23 +641,28 @@
             stats,
             stats,
             pltpu.VMEM((shards * rows, LANES), F32),
-            blocks,
-            blocks,
+            halves,
+            halves,
+            halves,
+            halves,
             pltpu.VMEM((rows, LANES), F32),
             pltpu.VMEM((width // LANES, LANES), F32),
-            pltpu.VMEM((shards, SUB, LANES), F32),
+            pltpu.VMEM((shards, LANES), F32),
+            pltpu.VMEM((shards * rows_dev, LANES), F32),
             pltpu.VMEM((rows, LANES), BF16),
             blocks,
             pltpu.VMEM((shards * rows_dev, width), BF16),
             pltpu.VMEM((shards * rows_dev, hidden), BF16),
-            blocks,
-            blocks,
+            halves,
+            halves,
+            halves,
+            halves,
             *(pltpu.VMEM(args[i].shape, args[i].dtype) for i in (0, 3, 4, 6)),
             pltpu.VMEM((width,), BF16),
             *(pltpu.VMEM(args[i].shape, args[i].dtype) for i in (12, 13)),
             pltpu.SemaphoreType.DMA((13,)),
-            pltpu.SemaphoreType.DMA((9, shards)),
-            pltpu.SemaphoreType.DMA((9, shards)),
+            pltpu.SemaphoreType.DMA((KINDS, shards)),
+            pltpu.SemaphoreType.DMA((KINDS, shards)),
         ],
         compiler_params=pltpu.CompilerParams(
             collective_id=0, has_side_effects=True, vmem_limit_bytes=60 * 1024 * 1024

time: 45.2 us -> 45.9 us (1.015)
  Pallas kernels: 42.9 us -> 43.7 us
    pallas_call x1, Pallas kernels: 42.9 us -> 43.7 us  [local(): pl.pallas_call(functools.partial(layer_kernel, shards), out_shape=jax.Sha...]
where the time goes in v3:
time: 45.9 us; the launch traced here: 45.7 us
  Pallas kernels  43.7 us (95%)
  local copies, waits for them, and re-layouts  1.33 us (3%)
  between operations  0.66 us (1%)
    pallas_call x1, Pallas kernels, local(): pl.pallas_call(functools.partial(layer_kernel, shards), out_shape=jax.Sha...  43.7 us
    unnamed x1, local copies, waits for them, and re-layouts  1.33 us

profile of v3, /device:TPU:0, one launch (start us, length us, event | category | flops | bytes accessed | tf_op | source)
XLA Modules:
  0.0 45.7 jit_solution(5218665446505696797)
XLA Ops:
  0.7 43.7 %shard_map.136 = bf16[3,2048]{1,0:T(4,128)(2,1)} custom-call(bf16[3,4096]{1,0:T(4,128)(2,1)} %q_hbm.1, bf16[128,512]{1,0:T(8,128)(2,1)} %ck_ref.1, bf16[128,512]{1,0:T(8,128)(2,1)} %cv_ref.1, bf16[3,512]{1,0:T(4,128)(2,1)} %nk_hbm.1, bf16[3,512]{1,0:T(4,128)(2,1)} %nv_hbm.1, s32[1]{0:T(128)S(6)} %copy.16.len_ref, bf16[3,2048]{1,0:T(4,128)(2,1)} %res_hbm.1, ...), custom_call_target="tpu_custom_call" | custom-call | flops 503316480 | bytes 9437184 | tf_op jit(solution)/shard_map/pallas_call | solution.py:620
  44.4 1.3 %copy.17 = bf16[3,2048]{1,0:T(4,128)(2,1)} copy(bf16[3,2048]{1,0:T(4,128)(2,1)} %shard_map.136) | data formatting | bytes 24576

commit v4 on v2

--- a/solution.py
+++ b/solution.py
@@ -206,6 +206,8 @@
     load_sem,
     send_sem,
     recv_sem,
+    send_all,
+    recv_all,
 ):
     me = lax.axis_index("ctx")
     team = shards // KV_HEADS
@@ -247,11 +249,11 @@
         pltpu.make_async_copy(src, dst, load_sem.at[i])
         for i, (src, dst) in enumerate(small + large)
     ]
-    for load in loads:
+    early = len(small) + 2
+    for load in loads[:early]:
         load.start()
     for load in loads[: len(small)]:
         load.wait()
-    loads = loads[len(small) :]
 
     q_wide[...] = jnp.zeros_like(q_wide)
     for one in range(HEADS):
@@ -297,18 +299,36 @@
 
     def peers(body):
         def step_body(step, carry):
-            body(lax.rem(me + step, shards))
+            side = 2 * (step % 2) - 1
+            body(lax.rem(me + shards // 2 + (step + 1) // 2 * side, shards))
             return carry
 
-        lax.fori_loop(1, shards, step_body, 0)
+        lax.fori_loop(0, shards - 1, step_body, 0)
+
+    def all_remote(kind, src, dst, target):
+        return pltpu.make_async_remote_copy(
+            src_ref=src,
+            dst_ref=dst,
+            send_sem=send_all.at[kind],
+            recv_sem=recv_all.at[kind],
+            device_id={"ctx": target},
+            device_id_type=MESH,
+        )
+
+    def wait_all(sem, kind, ref):
+        most = ref.at[pl.ds(0, shards - 1)]
+        pltpu.make_async_copy(most, most, sem.at[kind]).wait()
 
     def q_copy(target, source):
-        return remote(Q, q_send.at[target % team], q_recv.at[source], target, source)
+        return all_remote(Q, q_send.at[target % team], q_recv.at[source], target)
 
     peers(lambda other: q_copy(other, me).start())
     for step in range(1, team):
         for copy in key_copies(*near(step), mate):
             copy.start()
+    for load in loads[early:]:
+        load.start()
+    loads = loads[len(small) :]
 
     q_recv[me] = q_send[mate]
     new_recv[mate] = new_send[mate]
@@ -323,7 +343,7 @@
             jnp.sum(share, axis=1, keepdims=True), (rows_dev, LANES)
         )
 
-    peers(lambda other: q_copy(me, other).wait_recv())
+    wait_all(recv_all, Q, q_recv)
     gathered = q_recv[...].astype(F32).reshape(shards, team, SUB, LANES)
     for one in range(team):
         q_heads[one] = gathered[:, one].reshape(shards * SUB, LANES).astype(BF16)
@@ -435,11 +455,11 @@
     proj_send[...] = stage[...].reshape(proj_send.shape).astype(BF16)
 
     def proj_copy(target, source):
-        return remote(PROJ, proj_send.at[target], proj_recv.at[source], target, source)
+        return all_remote(PROJ, proj_send.at[target], proj_recv.at[source], target)
 
     peers(lambda other: proj_copy(other, me).start())
     proj_recv[me] = proj_send[me]
-    peers(lambda other: proj_copy(me, other).wait_recv())
+    wait_all(recv_all, PROJ, proj_recv)
     state = res_wide[...] + jnp.sum(proj_recv[...].astype(F32), axis=0)
     state = state.reshape(rows_dev, chunks, LANES)
     squares = jnp.sum(jnp.sum(state * state, axis=1, keepdims=True), axis=2, keepdims=True)
@@ -448,11 +468,11 @@
     row_send[...] = normed.astype(BF16)
 
     def row_copy(target, source):
-        return remote(ROWS, row_send, row_recv.at[source], target, source)
+        return all_remote(ROWS, row_send, row_recv.at[source], target)
 
     peers(lambda other: row_copy(other, me).start())
     row_recv[me] = row_send[...]
-    peers(lambda other: row_copy(me, other).wait_recv())
+    wait_all(recv_all, ROWS, row_recv)
 
     stage[...] = row_recv[...].astype(F32).reshape(stage.shape)
     for c in range(chunks):
@@ -476,7 +496,7 @@
     back_send[...] = stage[...].reshape(back_send.shape).astype(BF16)
 
     def back_copy(target, source):
-        return remote(BACK, back_send.at[target], back_recv.at[source], target, source)
+        return all_remote(BACK, back_send.at[target], back_recv.at[source], target)
 
     peers(lambda other: back_copy(other, me).start())
     back_recv[me] = back_send[me]
@@ -492,13 +512,10 @@
             for copy in head_copies(target, at, me, plane):
                 copy.wait_send()
 
-    def sent(other):
-        q_copy(other, me).wait_send()
-        proj_copy(other, me).wait_send()
-        row_copy(other, me).wait_send()
-
-    peers(sent)
-    peers(lambda other: back_copy(me, other).wait_recv())
+    wait_all(send_all, Q, q_recv)
+    wait_all(send_all, PROJ, proj_recv)
+    wait_all(send_all, ROWS, row_recv)
+    wait_all(recv_all, BACK, back_recv)
 
     def combine(e, total):
         block = back_recv[e].astype(F32).reshape(rows_dev, chunks, LANES)
@@ -512,7 +529,7 @@
         out_ref[:, c * LANES : (c + 1) * LANES] = res_wide[
             pl.ds(c, rows_dev, stride=chunks), :
         ].astype(BF16)
-    peers(lambda other: back_copy(other, me).wait_send())
+    wait_all(send_all, BACK, back_recv)
 
 
 def local(*args):
@@ -576,6 +593,8 @@
             pltpu.SemaphoreType.DMA((13,)),
             pltpu.SemaphoreType.DMA((9, shards)),
             pltpu.SemaphoreType.DMA((9, shards)),
+            pltpu.SemaphoreType.DMA((9,)),
+            pltpu.SemaphoreType.DMA((9,)),
         ],
         compiler_params=pltpu.CompilerParams(
             collective_id=0, has_side_effects=True, vmem_limit_bytes=60 * 1024 * 1024

time: 45.2 us -> 47.8 us (1.058)
  Pallas kernels: 42.9 us -> 45.5 us
    pallas_call x1, Pallas kernels: 42.9 us -> 45.5 us  [local(): pl.pallas_call(functools.partial(layer_kernel, shards), out_shape=jax.Sha...]
where the time goes in v4:
time: 47.8 us; the launch traced here: 47.5 us
  Pallas kernels  45.5 us (95%)
  local copies, waits for them, and re-layouts  1.33 us (3%)
  between operations  0.66 us (1%)
    pallas_call x1, Pallas kernels, local(): pl.pallas_call(functools.partial(layer_kernel, shards), out_shape=jax.Sha...  45.5 us
    unnamed x1, local copies, waits for them, and re-layouts  1.33 us

profile of v4, /device:TPU:0, one launch (start us, length us, event | category | flops | bytes accessed | tf_op | source)
XLA Modules:
  0.0 47.5 jit_solution(199513747240922454)
XLA Ops:
  0.7 45.5 %shard_map.136 = bf16[3,2048]{1,0:T(4,128)(2,1)} custom-call(bf16[3,4096]{1,0:T(4,128)(2,1)} %q_hbm.1, bf16[128,512]{1,0:T(8,128)(2,1)} %ck_ref.1, bf16[128,512]{1,0:T(8,128)(2,1)} %cv_ref.1, bf16[3,512]{1,0:T(4,128)(2,1)} %nk_hbm.1, bf16[3,512]{1,0:T(4,128)(2,1)} %nv_hbm.1, s32[1]{0:T(128)S(6)} %copy.16.len_ref, bf16[3,2048]{1,0:T(4,128)(2,1)} %res_hbm.1, ...), custom_call_target="tpu_custom_call" | custom-call | flops 503316480 | bytes 9437184 | tf_op jit(solution)/shard_map/pallas_call | solution.py:555
  46.2 1.3 %copy.17 = bf16[3,2048]{1,0:T(4,128)(2,1)} copy(bf16[3,2048]{1,0:T(4,128)(2,1)} %shard_map.136) | data formatting | bytes 24576

commit v5 on v3

--- a/solution.py
+++ b/solution.py
@@ -134,6 +134,10 @@
 KINDS = 12
 
 
+def shuffled(team, i):
+    return (i % 2) * (team // 2) + i // 2
+
+
 def fits(shards, rows_dev, width, capacity, experts_dev):
     team = shards // KV_HEADS
     if shards % KV_HEADS or team == 0 or (HEADS // KV_HEADS) % team:
@@ -142,6 +146,8 @@
     return (
         experts_dev == 1
         and team == KV_HEADS
+        and team % 2 == 0
+        and all(shuffled(team, shuffled(team, i)) == i for i in range(team))
         and HEAD_DIM == LANES
         and shards * SUB == LANES
         and (shards * rows_dev) % (2 * SUB) == 0
@@ -222,6 +228,8 @@
     chunks = width // LANES
     cache = ck_ref.shape[0]
     plane, mate = me // team, me % team
+    swap = functools.partial(shuffled, team)
+    head = swap(mate)
     chips = shards // 2
     chip, core = me // 2, me % 2
     sibling = me + 1 - 2 * core
@@ -236,7 +244,7 @@
 
     lax.fori_loop(1, shards, greet, 0)
 
-    own_lanes = pl.ds(pl.multiple_of(mate * LANES, LANES), LANES)
+    own_lanes = pl.ds(pl.multiple_of(head * LANES, LANES), LANES)
     small = [
         (q_hbm, q_ref),
         (nk_hbm, nk_ref),
@@ -258,11 +266,11 @@
         pltpu.make_async_copy(src, dst, load_sem.at[i])
         for i, (src, dst) in enumerate(small + large)
     ]
-    early = len(small) + 2
-    for load in loads[:early]:
+    for load in loads:
         load.start()
     for load in loads[: len(small)]:
         load.wait()
+    loads = loads[len(small) :]
 
     q_wide[...] = jnp.zeros_like(q_wide)
     for one in range(HEADS):
@@ -305,7 +313,8 @@
         other = lax.rem(mate + step, team)
         return other, plane * team + other
 
-    def key_copies(lane_head, target, source_mate):
+    def key_copies(target_mate, target, source_mate):
+        lane_head = swap(target_mate)
         lanes = pl.ds(pl.multiple_of(lane_head * LANES, LANES), LANES)
         source = plane * team + source_mate
         return (
@@ -324,18 +333,15 @@
         lax.fori_loop(1, shards, step_body, 0)
 
     def q_copy(target, source):
-        return remote(Q, q_send.at[target % team], q_recv.at[source], target, source)
+        return remote(Q, q_send.at[swap(target % team)], q_recv.at[source], target, source)
 
     peers(lambda other: q_copy(other, me).start())
     for step in range(1, team):
         for copy in key_copies(*near(step), mate):
             copy.start()
-    for load in loads[early:]:
-        load.start()
-    loads = loads[len(small) :]
-
-    q_recv[me] = q_send[mate]
-    new_recv[mate] = new_send[mate]
+
+    q_recv[me] = q_send[head]
+    new_recv[mate] = new_send[head]
 
     for c in range(chunks):
         lanes = slice(c * LANES, (c + 1) * LANES)
@@ -407,7 +413,7 @@
         num_send[to] = numer.astype(BF16)
         stat_send[to] = jnp.where(stat_row == 0, top, total)
 
-        target = mate * team + to
+        target = head * team + to
 
         @pl.when(target != me)
         def _():
@@ -423,7 +429,7 @@
 
     lax.fori_loop(0, team, attend, 0)
     for at in range(team):
-        source = at * team + plane
+        source = at * team + swap(plane)
 
         @pl.when(source != me)
         def _():
@@ -567,7 +573,7 @@
         for copy in key_copies(*near(step), mate):
             copy.wait_send()
     for at in range(team):
-        target = mate * team + at
+        target = head * team + at
 
         @pl.when(target != me)
         def _():

time: 45.9 us -> 43.7 us (0.952)
  Pallas kernels: 43.7 us -> 41.5 us
    pallas_call x1, Pallas kernels: 43.7 us -> 41.5 us  [local(): pl.pallas_call(functools.partial(layer_kernel, shards), out_shape=jax.Sha...]
where the time goes in v5:
time: 43.7 us; the launch traced here: 43.5 us
  Pallas kernels  41.5 us (95%)
  local copies, waits for them, and re-layouts  1.33 us (3%)
  between operations  0.66 us (2%)
    pallas_call x1, Pallas kernels, local(): pl.pallas_call(functools.partial(layer_kernel, shards), out_shape=jax.Sha...  41.5 us
    unnamed x1, local copies, waits for them, and re-layouts  1.33 us

profile of v5, /device:TPU:0, one launch (start us, length us, event | category | flops | bytes accessed | tf_op | source)
XLA Modules:
  0.0 43.5 jit_solution(7997063119392456639)
XLA Ops:
  0.7 41.5 %shard_map.136 = bf16[3,2048]{1,0:T(4,128)(2,1)} custom-call(bf16[3,4096]{1,0:T(4,128)(2,1)} %q_hbm.1, bf16[128,512]{1,0:T(8,128)(2,1)} %ck_ref.1, bf16[128,512]{1,0:T(8,128)(2,1)} %cv_ref.1, bf16[3,512]{1,0:T(4,128)(2,1)} %nk_hbm.1, bf16[3,512]{1,0:T(4,128)(2,1)} %nv_hbm.1, s32[1]{0:T(128)S(6)} %copy.16.len_ref, bf16[3,2048]{1,0:T(4,128)(2,1)} %res_hbm.1, ...), custom_call_target="tpu_custom_call" | custom-call | flops 503316480 | bytes 9437184 | tf_op jit(solution)/shard_map/pallas_call | solution.py:626
  42.2 1.3 %copy.17 = bf16[3,2048]{1,0:T(4,128)(2,1)} copy(bf16[3,2048]{1,0:T(4,128)(2,1)} %shard_map.136) | data formatting | bytes 24576

commit v6 on v5

--- a/solution.py
+++ b/solution.py
@@ -194,8 +194,6 @@
     stat_send,
     stat_recv,
     stage,
-    proj_away,
-    proj_near,
     proj_send,
     proj_recv,
     res_wide,
@@ -257,7 +255,7 @@
     large = [
         (ck_ref.at[:, own_lanes], k_all.at[mate]),
         (cv_ref.at[:, own_lanes], v_all.at[mate]),
-        (wo_ref, wo),
+        (wo_ref, wo.at[core]),
         (wg_ref.at[0], wg),
         (wu_ref.at[0], wu),
         (wd_ref.at[0], wd),
@@ -340,6 +338,11 @@
         for copy in key_copies(*near(step), mate):
             copy.start()
 
+    def weight_copy(target, source, source_core):
+        return remote(PROJ_PAIR, wo_ref, wo.at[source_core], target, source)
+
+    weight_copy(sibling, me, core).start()
+
     q_recv[me] = q_send[head]
     new_recv[mate] = new_send[head]
 
@@ -350,8 +353,12 @@
 
     peers(lambda other: q_copy(me, other).wait_recv())
     gathered = q_recv[...].astype(F32).reshape(shards, team, SUB, LANES)
+    split = gathered.reshape(chips, 2, team, SUB, LANES)
     for one in range(team):
-        q_heads[one] = gathered[:, one].reshape(shards * SUB, LANES).astype(BF16)
+        first = one // 2 * 2
+        q_heads[one] = (
+            split[:, one % 2, first : first + 2].reshape(shards * SUB, LANES).astype(BF16)
+        )
     at_lane = lax.broadcasted_iota(jnp.int32, (shards, LANES), 1)
     for r in range(rows_dev):
         both = gathered[:, r, SUB - 2, :] + gathered[:, r, SUB - 1, :]
@@ -378,10 +385,8 @@
     cache_ok = (spot < lengths).reshape(n_cache, LANES)
     lane = lax.broadcasted_iota(jnp.int32, (n_new, LANES), 1)
     place = lax.broadcasted_iota(jnp.int32, (n_new, LANES), 0)
-    row_of = (lane // SUB) * rows_dev + (lane % SUB) % rows_dev
     key_at = place % SUB
     span = (plane * team + place // SUB) * rows_dev + key_at
-    new_ok = (key_at < rows_dev) & (span <= row_of)
     across = (((1,), (1,)), ((), ()))
     down = (((0,), (0,)), ((), ()))
     scale = HEAD_DIM ** (-0.5)
@@ -396,6 +401,8 @@
     def attend(step, carry):
         to = lax.rem(plane + step, team)
         queries = q_heads[to]
+        owner = lane // (2 * SUB) * 2 + to % 2
+        new_ok = (key_at < rows_dev) & (span <= owner * rows_dev + (lane % SUB) % rows_dev)
         keys = k_all[...].reshape(n_cache, LANES)
         old = lax.dot_general(keys, queries, across, preferred_element_type=F32) * scale
         new = lax.dot_general(new_k, queries, across, preferred_element_type=F32) * scale
@@ -442,14 +449,13 @@
     attention = jnp.sum(num_recv[...].astype(F32) * weight, axis=0).astype(BF16)
 
     n_rows = shards * rows_dev
-    tile_row = lax.broadcasted_iota(jnp.int32, (n_rows, LANES), 0)
-    tile_lane = lax.broadcasted_iota(jnp.int32, (n_rows, LANES), 1)
-    tile_place = tile_row // rows_dev
-    tile_device = (tile_place % chips) * 2 + tile_place // chips
+    tile_row = lax.broadcasted_iota(jnp.int32, (n_rows // 2, LANES), 0)
+    tile_lane = lax.broadcasted_iota(jnp.int32, (n_rows // 2, LANES), 1)
     parts = []
-    for which in range(pair):
-        pick = (tile_device == tile_lane // SUB) & (
-            tile_lane % SUB == which * rows_dev + tile_row % rows_dev
+    for which in range(2 * pair):
+        place = which // pair * SUB + which % pair * rows_dev
+        pick = (tile_row // rows_dev == tile_lane // (2 * SUB)) & (
+            tile_lane % (2 * SUB) == place + tile_row % rows_dev
         )
         pick = jnp.where(pick, 1.0, 0.0).astype(BF16)
         parts.append(
@@ -459,14 +465,16 @@
 
     def spread(first, tile):
         for j in range(tile.shape[1] // LANES):
-            stage[pl.ds(first + j, n_rows, stride=chunks), :] = tile[
+            stage[pl.ds(first + j, tile.shape[0], stride=chunks), :] = tile[
                 :, j * LANES : (j + 1) * LANES
             ]
 
     loads[2].wait()
+    weight_copy(me, sibling, 1 - core).wait_recv()
     wide = 4 * LANES
     for at in range(width // wide):
-        tile = jnp.dot(columns, wo[:, at * wide : (at + 1) * wide], preferred_element_type=F32)
+        part = wo[:, :, at * wide : (at + 1) * wide].reshape(columns.shape[1], wide)
+        tile = jnp.dot(columns, part, preferred_element_type=F32)
         spread(4 * at, tile)
 
     half_rows = chips * rows_dev * chunks
@@ -480,35 +488,28 @@
 
         lax.fori_loop(1, chips, step_body, 0)
 
-    def reduce_copies(pair_kind, kind, away, near, send, recv):
-        def pair_copy(target, source):
-            return remote(pair_kind, away, near, target, source)
-
-        def copy(target_chip, source_chip):
-            return remote(
-                kind,
-                send.at[target_chip],
-                recv.at[source_chip],
-                target_chip * 2 + core,
-                source_chip * 2 + core,
-            )
-
-        return pair_copy, copy
-
-    def reduce_to_owners(copies, away, near, send, recv):
-        pair_copy, copy = copies
-        away[...] = stage[away_half, :].astype(BF16).reshape(away.shape)
-        pair_copy(sibling, me).start()
-        pair_copy(me, sibling).wait_recv()
-        total = stage[own_half, :].reshape(near.shape) + near[...].astype(F32)
-        send[...] = total.astype(BF16)
-        others(lambda other: copy(other, chip).start())
-        recv[chip] = send[chip]
-
-    proj_refs = (proj_away, proj_near, proj_send, proj_recv)
-    proj_copies = reduce_copies(PROJ_PAIR, PROJ, *proj_refs)
-    reduce_to_owners(proj_copies, *proj_refs)
-    others(lambda other: proj_copies[1](chip, other).wait_recv())
+    def chip_copy(kind, send, recv, target_chip, source_chip):
+        return remote(
+            kind,
+            send.at[target_chip],
+            recv.at[source_chip],
+            target_chip * 2 + core,
+            source_chip * 2 + core,
+        )
+
+    def proj_copy(target_chip, source_chip):
+        return chip_copy(PROJ, proj_send, proj_recv, target_chip, source_chip)
+
+    def back_copy(target_chip, source_chip):
+        return chip_copy(BACK, back_send, back_recv, target_chip, source_chip)
+
+    def back_pair_copy(target, source):
+        return remote(BACK_PAIR, back_away, back_near, target, source)
+
+    proj_send[...] = stage[0:half_rows, :].astype(BF16).reshape(proj_send.shape)
+    others(lambda other: proj_copy(other, chip).start())
+    proj_recv[chip] = proj_send[chip]
+    others(lambda other: proj_copy(chip, other).wait_recv())
     state = res_wide[...] + jnp.sum(proj_recv[...].astype(F32), axis=0)
     state = state.reshape(rows_dev, chunks, LANES)
     squares = jnp.sum(jnp.sum(state * state, axis=1, keepdims=True), axis=2, keepdims=True)
@@ -565,9 +566,13 @@
     for at in range(width // wide):
         tile = jnp.dot(act[...], wd[:, at * wide : (at + 1) * wide], preferred_element_type=F32)
         spread(4 * at, tile * jnp.concatenate([mix[...]] * 4, axis=1))
-    back_refs = (back_away, back_near, back_send, back_recv)
-    back_copies = reduce_copies(BACK_PAIR, BACK, *back_refs)
-    reduce_to_owners(back_copies, *back_refs)
+    back_away[...] = stage[away_half, :].astype(BF16).reshape(back_away.shape)
+    back_pair_copy(sibling, me).start()
+    back_pair_copy(me, sibling).wait_recv()
+    summed = stage[own_half, :].reshape(back_near.shape) + back_near[...].astype(F32)
+    back_send[...] = summed.astype(BF16)
+    others(lambda other: back_copy(other, chip).start())
+    back_recv[chip] = back_send[chip]
 
     for step in range(1, team):
         for copy in key_copies(*near(step), mate):
@@ -581,17 +586,17 @@
                 copy.wait_send()
 
     peers(lambda other: q_copy(other, me).wait_send())
-    proj_copies[0](sibling, me).wait_send()
-    back_copies[0](sibling, me).wait_send()
+    weight_copy(sibling, me, core).wait_send()
+    back_pair_copy(sibling, me).wait_send()
 
     def sent(other):
-        proj_copies[1](other, chip).wait_send()
+        proj_copy(other, chip).wait_send()
         row_copy(other * 2 + core, chip).wait_send()
         row_pair_copy(sibling, me, core * chips + other).wait_send()
 
     others(sent)
     row_pair_copy(sibling, me, core * chips + chip).wait_send()
-    others(lambda other: back_copies[1](chip, other).wait_recv())
+    others(lambda other: back_copy(chip, other).wait_recv())
     final = state + jnp.sum(back_recv[...].astype(F32), axis=0).reshape(state.shape)
     for r in range(rows_dev):
         res_wide[r * chunks : (r + 1) * chunks, :] = final[r]
@@ -599,7 +604,7 @@
         out_ref[:, c * LANES : (c + 1) * LANES] = res_wide[
             pl.ds(c, rows_dev, stride=chunks), :
         ].astype(BF16)
-    others(lambda other: back_copies[1](other, chip).wait_send())
+    others(lambda other: back_copy(other, chip).wait_send())
 
 
 def local(*args):
@@ -629,7 +634,7 @@
         in_specs=[any_spec] * 5 + [smem] + [any_spec] * 8,
         out_specs=vmem,
         scratch_shapes=[
-            pltpu.VMEM(out_weight.shape, BF16),
+            pltpu.VMEM((2, *out_weight.shape), BF16),
             pltpu.VMEM((width, hidden), BF16),
             pltpu.VMEM((width, hidden), BF16),
             pltpu.VMEM((hidden, width), BF16),
@@ -647,8 +652,6 @@
             stats,
             stats,
             pltpu.VMEM((shards * rows, LANES), F32),
-            halves,
-            halves,
             halves,
             halves,
             pltpu.VMEM((rows, LANES), F32),

time: 43.7 us -> 42.9 us (0.982)
  Pallas kernels: 41.5 us -> 40.7 us
    pallas_call x1, Pallas kernels: 41.5 us -> 40.7 us  [local(): pl.pallas_call(functools.partial(layer_kernel, shards), out_shape=jax.Sha...]
where the time goes in v6:
time: 42.9 us; the launch traced here: 42.7 us
  Pallas kernels  40.7 us (95%)
  local copies, waits for them, and re-layouts  1.33 us (3%)
  between operations  0.66 us (2%)
    pallas_call x1, Pallas kernels, local(): pl.pallas_call(functools.partial(layer_kernel, shards), out_shape=jax.Sha...  40.7 us
    unnamed x1, local copies, waits for them, and re-layouts  1.33 us

profile of v6, /device:TPU:0, one launch (start us, length us, event | category | flops | bytes accessed | tf_op | source)
XLA Modules:
  0.0 42.7 jit_solution(12727958073760094684)
XLA Ops:
  0.7 40.7 %shard_map.136 = bf16[3,2048]{1,0:T(4,128)(2,1)} custom-call(bf16[3,4096]{1,0:T(4,128)(2,1)} %q_hbm.1, bf16[128,512]{1,0:T(8,128)(2,1)} %ck_ref.1, bf16[128,512]{1,0:T(8,128)(2,1)} %cv_ref.1, bf16[3,512]{1,0:T(4,128)(2,1)} %nk_hbm.1, bf16[3,512]{1,0:T(4,128)(2,1)} %nv_hbm.1, s32[1]{0:T(128)S(6)} %copy.16.len_ref, bf16[3,2048]{1,0:T(4,128)(2,1)} %res_hbm.1, ...), custom_call_target="tpu_custom_call" | custom-call | flops 503316480 | bytes 9437184 | tf_op jit(solution)/shard_map/pallas_call | solution.py:631
  41.4 1.3 %copy.17 = bf16[3,2048]{1,0:T(4,128)(2,1)} copy(bf16[3,2048]{1,0:T(4,128)(2,1)} %shard_map.136) | data formatting | bytes 24576

commit v7 on v6

--- a/solution.py
+++ b/solution.py
@@ -186,6 +186,7 @@
     q_heads,
     k_all,
     v_all,
+    values_t,
     new_wide,
     new_send,
     new_recv,
@@ -392,6 +393,8 @@
     scale = HEAD_DIM ** (-0.5)
     stat_row = lax.broadcasted_iota(jnp.int32, (SUB, LANES), 0)
 
+    values_t[...] = v_all[...].reshape(n_cache, LANES).T
+
     def head_copies(target, target_mate, source, source_plane):
         return (
             remote(NUM, num_send.at[target_mate], num_recv.at[source_plane], target, source),
@@ -414,8 +417,7 @@
         old = jnp.where(cache_ok, jnp.exp(old - top), 0.0)
         new = jnp.where(new_ok, jnp.exp(new - top), 0.0)
         total = jnp.sum(old, axis=0, keepdims=True) + jnp.sum(new, axis=0, keepdims=True)
-        values = v_all[...].reshape(n_cache, LANES)
-        numer = lax.dot_general(values, old.astype(BF16), down, preferred_element_type=F32)
+        numer = jnp.dot(values_t[...], old.astype(BF16), preferred_element_type=F32)
         numer += lax.dot_general(new_v, new.astype(BF16), down, preferred_element_type=F32)
         num_send[to] = numer.astype(BF16)
         stat_send[to] = jnp.where(stat_row == 0, top, total)
@@ -603,7 +605,7 @@
     for c in range(chunks):
         out_ref[:, c * LANES : (c + 1) * LANES] = res_wide[
             pl.ds(c, rows_dev, stride=chunks), :
-        ].astype(BF16)
+        ]
     others(lambda other: back_copy(other, chip).wait_send())
 
 
@@ -630,7 +632,7 @@
     flops = 2 * shards * rows_dev * width * (3 * hidden + out_weight.shape[0])
     return pl.pallas_call(
         functools.partial(layer_kernel, shards),
-        out_shape=jax.ShapeDtypeStruct((rows_dev, width), BF16),
+        out_shape=jax.ShapeDtypeStruct((rows_dev, width), F32),
         in_specs=[any_spec] * 5 + [smem] + [any_spec] * 8,
         out_specs=vmem,
         scratch_shapes=[
@@ -644,6 +646,7 @@
             pltpu.VMEM((team, shards * SUB, LANES), BF16),
             keys,
             keys,
+            pltpu.VMEM((LANES, team * cache), BF16),
             pltpu.VMEM((KV_HEADS, 2 * SUB, LANES), F32),
             new,
             new,
@@ -679,7 +682,7 @@
         cost_estimate=pl.CostEstimate(
             flops=flops, bytes_accessed=2 * 3 * hidden * width, transcendentals=0
         ),
-    )(*args)
+    )(*args).astype(BF16)
 
 
 def solution(mesh):

time: 42.9 us -> 43 us (level)
  other arithmetic: 0 us -> 1.37 us
  local copies, waits for them, and re-layouts: 1.33 us -> 0 us
    convert_element_type x0 -> x1, other arithmetic: none -> 1.37 us  [local(): return pl.pallas_call(functools.partial(layer_kernel, shards), out_shape=...]
    unnamed x1 -> x0, local copies, waits for them, and re-layouts: 1.33 us -> none
where the time goes in v7:
time: 43 us; the launch traced here: 42.8 us
  Pallas kernels  40.8 us (95%)
  other arithmetic  1.37 us (3%)
  between operations  0.66 us (2%)
    pallas_call x1, Pallas kernels, local(): pl.pallas_call(functools.partial(layer_kernel, shards), out_shape=jax.Sha...  40.8 us
    convert_element_type x1, other arithmetic, local(): return pl.pallas_call(functools.partial(layer_kernel, shards), out_shape=...  1.37 us

profile of v7, /device:TPU:0, one launch (start us, length us, event | category | flops | bytes accessed | tf_op | source)
XLA Modules:
  0.0 42.8 jit_solution(13000602880516073731)
XLA Ops:
  0.7 40.8 %shard_map.136 = f32[3,2048]{1,0:T(4,128)} custom-call(bf16[3,4096]{1,0:T(4,128)(2,1)} %q_hbm.1, bf16[128,512]{1,0:T(8,128)(2,1)} %ck_ref.1, bf16[128,512]{1,0:T(8,128)(2,1)} %cv_ref.1, bf16[3,512]{1,0:T(4,128)(2,1)} %nk_hbm.1, bf16[3,512]{1,0:T(4,128)(2,1)} %nv_hbm.1, s32[1]{0:T(128)S(6)} %copy.15.len_ref, bf16[3,2048]{1,0:T(4,128)(2,1)} %res_hbm.1, ...), custom_call_target="tpu_custom_call" | custom-call | flops 503316480 | bytes 9437184 | tf_op jit(solution)/shard_map/pallas_call | solution.py:633
  41.5 1.4 %convert_element_type.3 = bf16[3,2048]{1,0:T(4,128)(2,1)} convert(f32[3,2048]{1,0:T(4,128)} %shard_map.136) | non-fusion elementwise | flops 6144 | bytes 36864 | tf_op jit(solution)/shard_map/convert_element_type | solution.py:685
